TPU v7x, 32 devices: a whole 2x2x4 slice. The times are simulated.
32 devices in a mesh: group: 4 (over x, core), blk: 8 (over z, y).
Axes of the slice: x: 2, y: 2, z: 4, core: 2. Of those that a mesh axis runs over, the one named last changes fastest.
Arguments:
- orbitals: float32 [32, 64, 4096], P(('group', 'blk')), may hold values from -6 to 6
- occupation: float32 [32], P(('group', 'blk')), may hold values from 0.3 to 1
Outputs:
- exchange: float32 [32, 64, 4096], P(('group', 'blk'))
All inputs are finite; a program needn't handle non-finite values.
Results may differ from a plain program's by a relative error of at most 0.0003.
Values sent between devices are 32-bit elements; how exact they have to be, the bound alone decides.
A program may use at most 128 MiB of HBM per device.

v0:
```python
import jax
import jax.numpy as jnp
from jax import lax
from jax.sharding import PartitionSpec as P

STEPS = 3


HIGH = lax.Precision.HIGHEST


def from_behind(value, axis, steps):
    count = lax.axis_size(axis)
    pairs = [(source, (source + steps) % count) for source in range(count)]
    return lax.ppermute(value, axis, pairs)


def tables(size):
    index = jnp.arange(size, dtype=jnp.int32)
    product = index[:, None] * index[None, :] % size
    angle = product.astype(jnp.float32) * (2.0 * jnp.pi / size)
    cosine = jnp.cos(angle)
    sine = jnp.sin(angle)
    forward = jnp.stack([jnp.stack([cosine, sine]), jnp.stack([-sine, cosine])])
    inverse = jnp.stack([jnp.stack([cosine, -sine]), jnp.stack([sine, cosine])])
    signed = jnp.where(index < size // 2, index, index - size).astype(jnp.float32)
    square = signed * signed
    total = square[:, None, None] + square[None, :, None] + square[None, None, :]
    step = 2.0 * jnp.pi / size
    kernel = jnp.pi / (step * step * total + 0.25)
    return (forward, inverse, kernel)


def complex_along(table, field, axis):
    if axis == 0:
        return jnp.einsum("rska,spabc->rpkbc", table, field, precision=HIGH)
    if axis == 1:
        return jnp.einsum("rskb,spabc->rpakc", table, field, precision=HIGH)
    return jnp.einsum("rskc,spabc->rpabk", table, field, precision=HIGH)


def solve_pairs(home, visit, forward, inverse, kernel):
    size = home.shape[1]
    count = home.shape[0]
    density = (home[:, None] * visit[None, :]).reshape(count * count, size, size, size)
    field = jnp.einsum("rka,pabc->rpkbc", forward[:, 0], density, precision=HIGH)
    field = complex_along(forward, field, 1)
    field = complex_along(forward, field, 2)
    field = field * kernel
    field = complex_along(inverse, field, 0)
    field = complex_along(inverse, field, 1)
    final = jnp.einsum("skc,spabc->pabk", inverse[0], field, precision=HIGH)
    final = final * (1.0 / (size * size * size))
    return final.reshape(count, count, size, size * size)


def local(orbitals, occupation):
    size = orbitals.shape[1]
    forward, inverse, kernel = tables(size)
    home_acc = jnp.zeros(orbitals.shape, jnp.float32)

    def meet_home(home_acc, visit_orb, visit_occ):
        potential = solve_pairs(orbitals, visit_orb, forward, inverse, kernel)
        home_acc = home_acc - jnp.sum(
            visit_occ[None, :, None, None] * visit_orb[None, :] * potential, axis=1
        )
        return (home_acc, potential)

    def collect(visit_acc, potential):
        return visit_acc - jnp.sum(
            occupation[:, None, None, None] * orbitals[:, None] * potential, axis=0
        )

    visit_acc = jnp.zeros(orbitals.shape, jnp.float32)
    visit_orb, visit_occ = (orbitals, occupation)
    for turn in range(STEPS):
        visit_orb, visit_occ = from_behind((visit_orb, visit_occ), "blk", 1)
        if turn > 0:
            visit_acc = from_behind(visit_acc, "blk", 1)
        home_acc, potential = meet_home(home_acc, visit_orb, visit_occ)
        visit_acc = collect(visit_acc, potential)
    visit_orb, visit_occ = from_behind((visit_orb, visit_occ), "group", 1)
    visit_acc = from_behind(visit_acc, "group", 1)
    home_acc, potential = meet_home(home_acc, visit_orb, visit_occ)
    visit_acc = collect(visit_acc, potential)
    visit_acc = from_behind(visit_acc, "group", -1)
    visit_acc = from_behind(visit_acc, "blk", -STEPS)
    return home_acc + visit_acc


def solution(mesh):
    return jax.shard_map(
        local,
        mesh=mesh,
        in_specs=(P(("group", "blk"), None, None), P(("group", "blk"))),
        out_specs=P(("group", "blk"), None, None),
        check_vma=False,
    )
```

profile of v0, /device:TPU:9, one launch (start us, length us, event | category | flops | bytes accessed | tf_op | source)
XLA Modules:
  0.0 396.8 jit_solution(17816211092330103329)
XLA Ops:
  0.0 1.2 collective-permute-start.1
  1.2 23.9 %collective-permute-done.1 = f32[1,64,4096]{2,1,0:T(8,128)S(1)} collective-permute-done((f32[1,64,4096]{2,1,0:T(8,128)}, f32[1,64,4096]{2,1,0:T(8,128)S(1)}, u32[]{:S(2)}, u32[]{:S(2)}) %collective-permute-start.1) | collective-permute-done | bytes 1048608 | tf_op jit(solution)/shard_map/ppermute | solution.py:15
  25.1 0.3 collective-permute-start.3
  26.2 0.1 fusion.94
  26.3 0.1 fusion.92
  26.6 0.6 add_divide_fusion
  27.2 21.9 %collective-permute-done.3 = f32[1,64,4096]{2,1,0:T(8,128)S(1)} collective-permute-done((f32[1,64,4096]{2,1,0:T(8,128)S(1)}, f32[1,64,4096]{2,1,0:T(8,128)S(1)}, u32[]{:S(2)}, u32[]{:S(2)}) %collective-permute-start.3) | collective-permute-done | bytes 1048608 | tf_op jit(solution)/shard_map/ppermute | solution.py:15
  49.1 2.8 fusion.106
  51.9 3.2 copy.89
  55.2 2.0 copy.80
  57.1 7.0 %convolution_bitcast_fusion.3 = f32[2,64,64,64,1]{1,3,0,2,4:T(8,128)} fusion(f32[64,64,64,1]{0,2,3,1:T(8,128)} %bitcast.339, f32[2,64,64,1]{2,1,0,3:T(8,128)S(1)} %fusion.80), kind=kOutput, calls=%fused_computation.39 | convolution fusion | flops 402653184 | bytes 3178496 | tf_op jit(solution)/shard_map/rka,pabc->rpkbc/dot_general | solution.py:46
  64.1 6.4 %copy.37 = f32[2,64,64,64,1]{2,3,0,4,1:T(8,128)} copy(f32[2,64,64,64,1]{1,3,0,2,4:T(8,128)} %convolution_bitcast_fusion.3) | data formatting | bytes 4194304 | tf_op jit(solution)/shard_map/reshape.3
  70.5 5.7 %fusion.66 = f32[64,64,2,64,1]{3,1,4,2,0:T(8,128)S(1)} fusion(f32[2,64,64,64,1]{2,3,0,4,1:T(8,128)} %copy.37, f32[1,2,64,64]{3,2,0,1:T(8,128)S(1)} %get-tuple-element.11, f32[1,2,64,64]{3,2,0,1:T(8,128)S(1)} %get-tuple-element.14), kind=kOutput, calls=%fused_computation.64 | convolution fusion | flops 805322752 | bytes 4259840 | tf_op jit(solution)/shard_map/rskb,spabc->rpakc/dot_general | solution.py:38
  76.2 7.2 %fusion.27 = f32[2,64,64,64,1]{3,2,0,1,4:T(8,128)S(1)} fusion(f32[64,64,2,64,1]{3,1,4,2,0:T(8,128)S(1)} %fusion.66, f32[64,64,64]{2,1,0:T(8,128)S(1)} %add_divide_fusion, f32[1,2,64,64]{3,2,0,1:T(8,128)S(1)} %get-tuple-element.11, f32[1,2,64,64]{3,2,0,1:T(8,128)S(1)} %get-tuple-element.14), kind=kOutput, calls=%fused_computation.31 | convolution fusion | flops 805847040 | bytes 5308416 | tf_op jit(solution)/shard_map/rskc,spabc->rpabk/dot_general | solution.py:39
  83.4 12.1 %fusion.28 = f32[2,64,64,64,1]{1,3,0,2,4:T(8,128)} fusion(f32[2,64,64,64,1]{3,2,0,1,4:T(8,128)S(1)} %fusion.27, f32[1,2,64,64]{3,2,1,0:T(8,128)S(1)} %get-tuple-element.15, f32[1,2,64,64]{3,2,1,0:T(8,128)S(1)} %get-tuple-element.10), kind=kOutput, calls=%fused_computation.32 | convolution fusion | flops 805322752 | bytes 4259840 | tf_op jit(solution)/shard_map/rska,spabc->rpkbc/dot_general | solution.py:36
  95.5 6.1 %copy.43 = f32[2,64,64,64,1]{2,3,0,4,1:T(8,128)} copy(f32[2,64,64,64,1]{1,3,0,2,4:T(8,128)} %fusion.28) | data formatting | bytes 4194304 | tf_op jit(solution)/shard_map/reshape.20
  101.6 6.0 %fusion.104 = f32[64,64,2,64,1]{3,1,4,2,0:T(8,128)S(1)} fusion(f32[2,64,64,64,1]{2,3,0,4,1:T(8,128)} %copy.43, f32[1,2,64,64]{3,2,1,0:T(8,128)S(1)} %get-tuple-element.15, f32[1,2,64,64]{3,2,1,0:T(8,128)S(1)} %get-tuple-element.10), kind=kOutput, calls=%fused_computation.111 | convolution fusion | flops 805322752 | bytes 4259840 | tf_op jit(solution)/shard_map/rskb,spabc->rpakc/dot_general | solution.py:38
  107.6 8.4 %bitcast_multiply_fusion.7 = f32[64,64,64]{2,1,0:T(8,128)} fusion(f32[64,64,2,64,1]{3,1,4,2,0:T(8,128)S(1)} %fusion.104, f32[1,64,64]{2,1,0:T(8,128)S(1)} %get-tuple-element.17, f32[1,64,64]{2,1,0:T(8,128)S(1)} %fusion.94), kind=kOutput, calls=%fused_computation.43 | convolution fusion | flops 402923520 | bytes 3178496 | tf_op jit(solution)/shard_map/skc,spabc->pabk/dot_general | solution.py:52
  116.0 2.9 reshape.400
  118.9 2.5 multiply_subtract_fusion.3
  121.3 5.1 %convolution_bitcast_fusion.2 = f32[2,64,64,64,1]{1,3,0,2,4:T(8,128)} fusion(f32[64,64,64,1]{0,2,3,1:T(8,128)S(1)} %bitcast.337, f32[2,64,64,1]{2,1,0,3:T(8,128)S(1)} %fusion.80), kind=kOutput, calls=%fused_computation.38 | convolution fusion | flops 402653184 | bytes 3178496 | tf_op jit(solution)/shard_map/rka,pabc->rpkbc/dot_general | solution.py:46
  126.4 6.1 %copy.48 = f32[2,64,64,64,1]{2,3,0,4,1:T(8,128)} copy(f32[2,64,64,64,1]{1,3,0,2,4:T(8,128)} %convolution_bitcast_fusion.2) | data formatting | bytes 4194304 | tf_op jit(solution)/shard_map/reshape.28
  132.5 2.5 collective-permute-start.8
  134.9 5.9 %fusion.63 = f32[64,64,2,64,1]{3,1,4,2,0:T(8,128)S(1)} fusion(f32[2,64,64,64,1]{2,3,0,4,1:T(8,128)} %copy.48, f32[1,2,64,64]{3,2,0,1:T(8,128)S(1)} %get-tuple-element.11, f32[1,2,64,64]{3,2,0,1:T(8,128)S(1)} %get-tuple-element.14), kind=kOutput, calls=%fused_computation.61 | convolution fusion | flops 805322752 | bytes 4259840 | tf_op jit(solution)/shard_map/rskb,spabc->rpakc/dot_general | solution.py:38
  140.9 7.2 %fusion.24 = f32[2,64,64,64,1]{3,2,0,1,4:T(8,128)S(1)} fusion(f32[64,64,2,64,1]{3,1,4,2,0:T(8,128)S(1)} %fusion.63, f32[64,64,64]{2,1,0:T(8,128)S(1)} %add_divide_fusion, f32[1,2,64,64]{3,2,0,1:T(8,128)S(1)} %get-tuple-element.11, f32[1,2,64,64]{3,2,0,1:T(8,128)S(1)} %get-tuple-element.14), kind=kOutput, calls=%fused_computation.27 | convolution fusion | flops 805847040 | bytes 5308416 | tf_op jit(solution)/shard_map/rskc,spabc->rpabk/dot_general | solution.py:39
  148.1 4.2 %collective-permute-start.7 = (f32[1,64,4096]{2,1,0:T(8,128)}, f32[1,64,4096]{2,1,0:T(8,128)}, u32[]{:S(2)}, u32[]{:S(2)}) collective-permute-start(f32[1,64,4096]{2,1,0:T(8,128)} %collective-permute-done.5), channel_id=1, source_target_pairs={{0,8},{8,16},{16,24},{24,0},{1,9},{9,17},{17,25},{25,1},{2,10},{10... | collective-permute-start | bytes 3145736 | tf_op jit(solution)/shard_map/ppermute | solution.py:15
  152.2 11.8 %fusion.31 = f32[2,64,64,64,1]{1,3,0,2,4:T(8,128)} fusion(f32[2,64,64,64,1]{3,2,0,1,4:T(8,128)S(1)} %fusion.24, f32[1,2,64,64]{3,2,1,0:T(8,128)S(1)} %get-tuple-element.15, f32[1,2,64,64]{3,2,1,0:T(8,128)S(1)} %get-tuple-element.10), kind=kOutput, calls=%fused_computation.33 | convolution fusion | flops 805322752 | bytes 4259840 | tf_op jit(solution)/shard_map/rska,spabc->rpkbc/dot_general | solution.py:36
  164.0 6.1 %copy.54 = f32[2,64,64,64,1]{2,3,0,4,1:T(8,128)} copy(f32[2,64,64,64,1]{1,3,0,2,4:T(8,128)} %fusion.31) | data formatting | bytes 4194304 | tf_op jit(solution)/shard_map/reshape.35
  170.1 6.3 %fusion.103 = f32[64,64,2,64,1]{3,1,4,2,0:T(8,128)S(1)} fusion(f32[2,64,64,64,1]{2,3,0,4,1:T(8,128)} %copy.54, f32[1,2,64,64]{3,2,1,0:T(8,128)S(1)} %get-tuple-element.15, f32[1,2,64,64]{3,2,1,0:T(8,128)S(1)} %get-tuple-element.10), kind=kOutput, calls=%fused_computation.110 | convolution fusion | flops 805322752 | bytes 4259840 | tf_op jit(solution)/shard_map/rskb,spabc->rpakc/dot_general | solution.py:38
  176.4 8.4 %bitcast_multiply_fusion.6 = f32[64,64,64]{2,1,0:T(8,128)} fusion(f32[64,64,2,64,1]{3,1,4,2,0:T(8,128)S(1)} %fusion.103, f32[1,64,64]{2,1,0:T(8,128)S(1)} %get-tuple-element.17, f32[1,64,64]{2,1,0:T(8,128)S(1)} %fusion.94), kind=kOutput, calls=%fused_computation.42 | convolution fusion | flops 402923520 | bytes 3178496 | tf_op jit(solution)/shard_map/skc,spabc->pabk/dot_general | solution.py:52
  184.8 3.1 reshape.406
  187.9 4.0 %fusion.105 = (f32[1,64,4096]{2,1,0:T(8,128)}, f32[1,64,4096]{2,1,0:T(8,128)}, f32[1,64,4096]{2,1,0:T(8,128)}) fusion(f32[1,64,4096]{2,1,0:T(8,128)S(1)} %copy-done, f32[1,64,4096]{2,1,0:T(8,128)} %collective-permute-done.7, f32[1,64,4096]{2,1,0:T(8,128)} %collective-permute-done.8, f32[1,64,4096]{2,1,0:T(8,128)} %reshape.406, f32[]{:T(128)} %bitcast.334, ...), kind=kLoop, calls=%fused_computation.112 | loop fusion | flops 1310720 | bytes 8388612 | tf_op jit(solution)/shard_map/mul | solution.py:45
  191.9 3.2 copy.107
  195.1 3.2 copy.98
  198.3 7.0 %convolution_bitcast_fusion.1 = f32[2,64,64,64,1]{1,3,0,2,4:T(8,128)} fusion(f32[64,64,64,1]{0,2,3,1:T(8,128)} %bitcast.340, f32[2,64,64,1]{2,1,0,3:T(8,128)S(1)} %fusion.80), kind=kOutput, calls=%fused_computation.37 | convolution fusion | flops 402653184 | bytes 3178496 | tf_op jit(solution)/shard_map/rka,pabc->rpkbc/dot_general | solution.py:46
  205.3 6.1 %copy.59 = f32[2,64,64,64,1]{2,3,0,4,1:T(8,128)} copy(f32[2,64,64,64,1]{1,3,0,2,4:T(8,128)} %convolution_bitcast_fusion.1) | data formatting | bytes 4194304 | tf_op jit(solution)/shard_map/reshape.43
  211.4 5.9 %fusion.60 = f32[64,64,2,64,1]{3,1,4,2,0:T(8,128)S(1)} fusion(f32[2,64,64,64,1]{2,3,0,4,1:T(8,128)} %copy.59, f32[1,2,64,64]{3,2,0,1:T(8,128)S(1)} %get-tuple-element.11, f32[1,2,64,64]{3,2,0,1:T(8,128)S(1)} %get-tuple-element.14), kind=kOutput, calls=%fused_computation.58 | convolution fusion | flops 805322752 | bytes 4259840 | tf_op jit(solution)/shard_map/rskb,spabc->rpakc/dot_general | solution.py:38
  217.3 7.2 %fusion.21 = f32[2,64,64,64,1]{3,2,0,1,4:T(8,128)S(1)} fusion(f32[64,64,2,64,1]{3,1,4,2,0:T(8,128)S(1)} %fusion.60, f32[64,64,64]{2,1,0:T(8,128)S(1)} %add_divide_fusion, f32[1,2,64,64]{3,2,0,1:T(8,128)S(1)} %get-tuple-element.11, f32[1,2,64,64]{3,2,0,1:T(8,128)S(1)} %get-tuple-element.14), kind=kOutput, calls=%fused_computation.23 | convolution fusion | flops 805847040 | bytes 5308416 | tf_op jit(solution)/shard_map/rskc,spabc->rpabk/dot_general | solution.py:39
  224.5 11.8 %fusion.34 = f32[2,64,64,64,1]{1,3,0,2,4:T(8,128)} fusion(f32[2,64,64,64,1]{3,2,0,1,4:T(8,128)S(1)} %fusion.21, f32[1,2,64,64]{3,2,1,0:T(8,128)S(1)} %get-tuple-element.15, f32[1,2,64,64]{3,2,1,0:T(8,128)S(1)} %get-tuple-element.10), kind=kOutput, calls=%fused_computation.34 | convolution fusion | flops 805322752 | bytes 4259840 | tf_op jit(solution)/shard_map/rska,spabc->rpkbc/dot_general | solution.py:36
  236.3 6.1 %copy.65 = f32[2,64,64,64,1]{2,3,0,4,1:T(8,128)} copy(f32[2,64,64,64,1]{1,3,0,2,4:T(8,128)} %fusion.34) | data formatting | bytes 4194304 | tf_op jit(solution)/shard_map/reshape.49
  242.4 6.1 %fusion.102 = f32[64,64,2,64,1]{3,1,4,2,0:T(8,128)S(1)} fusion(f32[2,64,64,64,1]{2,3,0,4,1:T(8,128)} %copy.65, f32[1,2,64,64]{3,2,1,0:T(8,128)S(1)} %get-tuple-element.15, f32[1,2,64,64]{3,2,1,0:T(8,128)S(1)} %get-tuple-element.10), kind=kOutput, calls=%fused_computation.109 | convolution fusion | flops 805322752 | bytes 4259840 | tf_op jit(solution)/shard_map/rskb,spabc->rpakc/dot_general | solution.py:38
  248.6 8.4 %bitcast_multiply_fusion.5 = f32[64,64,64]{2,1,0:T(8,128)} fusion(f32[64,64,2,64,1]{3,1,4,2,0:T(8,128)S(1)} %fusion.102, f32[1,64,64]{2,1,0:T(8,128)S(1)} %get-tuple-element.17, f32[1,64,64]{2,1,0:T(8,128)S(1)} %fusion.94), kind=kOutput, calls=%fused_computation.41 | convolution fusion | flops 402923520 | bytes 3178496 | tf_op jit(solution)/shard_map/skc,spabc->pabk/dot_general | solution.py:52
  257.0 5.6 %convolution_bitcast_fusion = f32[2,64,64,64,1]{1,3,0,2,4:T(8,128)} fusion(f32[64,64,64,1]{0,2,3,1:T(8,128)S(1)} %bitcast.338, f32[2,64,64,1]{2,1,0,3:T(8,128)S(1)} %fusion.80), kind=kOutput, calls=%fused_computation.36 | convolution fusion | flops 402653184 | bytes 3178496 | tf_op jit(solution)/shard_map/rka,pabc->rpkbc/dot_general | solution.py:46
  262.6 6.1 %copy.70 = f32[2,64,64,64,1]{2,3,0,4,1:T(8,128)} copy(f32[2,64,64,64,1]{1,3,0,2,4:T(8,128)} %convolution_bitcast_fusion) | data formatting | bytes 4194304 | tf_op jit(solution)/shard_map/reshape.57
  268.6 3.0 reshape.412
  271.6 5.9 %fusion.57 = f32[64,64,2,64,1]{3,1,4,2,0:T(8,128)S(1)} fusion(f32[2,64,64,64,1]{2,3,0,4,1:T(8,128)} %copy.70, f32[1,2,64,64]{3,2,0,1:T(8,128)S(1)} %get-tuple-element.11, f32[1,2,64,64]{3,2,0,1:T(8,128)S(1)} %get-tuple-element.14), kind=kOutput, calls=%fused_computation.55 | convolution fusion | flops 805322752 | bytes 4259840 | tf_op jit(solution)/shard_map/rskb,spabc->rpakc/dot_general | solution.py:38
  277.5 7.2 %fusion.18 = f32[2,64,64,64,1]{3,2,0,1,4:T(8,128)S(1)} fusion(f32[64,64,2,64,1]{3,1,4,2,0:T(8,128)S(1)} %fusion.57, f32[64,64,64]{2,1,0:T(8,128)S(1)} %add_divide_fusion, f32[1,2,64,64]{3,2,0,1:T(8,128)S(1)} %get-tuple-element.11, f32[1,2,64,64]{3,2,0,1:T(8,128)S(1)} %get-tuple-element.14), kind=kOutput, calls=%fused_computation.19 | convolution fusion | flops 805847040 | bytes 5308416 | tf_op jit(solution)/shard_map/rskc,spabc->rpabk/dot_general | solution.py:39
  284.7 2.4 multiply_subtract_fusion.1
  287.2 11.7 %fusion.37 = f32[2,64,64,64,1]{1,3,0,2,4:T(8,128)} fusion(f32[2,64,64,64,1]{3,2,0,1,4:T(8,128)S(1)} %fusion.18, f32[1,2,64,64]{3,2,1,0:T(8,128)S(1)} %get-tuple-element.15, f32[1,2,64,64]{3,2,1,0:T(8,128)S(1)} %get-tuple-element.10), kind=kOutput, calls=%fused_computation.35 | convolution fusion | flops 805322752 | bytes 4259840 | tf_op jit(solution)/shard_map/rska,spabc->rpkbc/dot_general | solution.py:36
  298.9 6.1 %copy.76 = f32[2,64,64,64,1]{2,3,0,4,1:T(8,128)} copy(f32[2,64,64,64,1]{1,3,0,2,4:T(8,128)} %fusion.37) | data formatting | bytes 4194304 | tf_op jit(solution)/shard_map/reshape.63
  305.0 6.1 %fusion.101 = f32[64,64,2,64,1]{3,1,4,2,0:T(8,128)S(1)} fusion(f32[2,64,64,64,1]{2,3,0,4,1:T(8,128)} %copy.76, f32[1,2,64,64]{3,2,1,0:T(8,128)S(1)} %get-tuple-element.15, f32[1,2,64,64]{3,2,1,0:T(8,128)S(1)} %get-tuple-element.10), kind=kOutput, calls=%fused_computation.108 | convolution fusion | flops 805322752 | bytes 4259840 | tf_op jit(solution)/shard_map/rskb,spabc->rpakc/dot_general | solution.py:38
  311.1 8.4 %bitcast_multiply_fusion.4 = f32[64,64,64]{2,1,0:T(8,128)} fusion(f32[64,64,2,64,1]{3,1,4,2,0:T(8,128)S(1)} %fusion.101, f32[1,64,64]{2,1,0:T(8,128)S(1)} %get-tuple-element.17, f32[1,64,64]{2,1,0:T(8,128)S(1)} %fusion.94), kind=kOutput, calls=%fused_computation.40 | convolution fusion | flops 402923520 | bytes 3178496 | tf_op jit(solution)/shard_map/skc,spabc->pabk/dot_general | solution.py:52
  319.5 3.1 reshape.418
  322.6 1.8 multiply_subtract_fusion
  324.4 0.5 collective-permute-start.11
  324.9 13.8 %collective-permute-done.11 = f32[1,64,4096]{2,1,0:T(8,128)S(1)} collective-permute-done((f32[1,64,4096]{2,1,0:T(8,128)S(1)}, f32[1,64,4096]{2,1,0:T(8,128)S(1)}, u32[]{:S(2)}, u32[]{:S(2)}) %collective-permute-start.11) | collective-permute-done | bytes 1048608 | tf_op jit(solution)/shard_map/ppermute | solution.py:15
  338.7 9.0 %collective-permute-start.12 = (f32[1,64,4096]{2,1,0:T(8,128)S(1)}, f32[1,64,4096]{2,1,0:T(8,128)S(1)}, u32[]{:S(2)}, u32[]{:S(2)}) collective-permute-start(f32[1,64,4096]{2,1,0:T(8,128)S(1)} %collective-permute-done.11), channel_id=1, source_target_pairs={{0,5},{1,6},{2,7},{3,0},{4,1},{5,2},{6,3},{7,4},{8,13},{9,14},{10,... | collective-permute-start | bytes 3145736 | tf_op jit(solution)/shard_map/ppermute | solution.py:15
  347.7 20.6 %collective-permute-done = f32[1]{0:T(128)} collective-permute-done((f32[1]{0:T(128)}, f32[1]{0:T(128)}, u32[]{:S(2)}, u32[]{:S(2)}) %collective-permute-start) | collective-permute-done | bytes 36 | tf_op jit(solution)/shard_map/ppermute | solution.py:15
  368.3 3.3 collective-permute-done.2
  371.6 3.3 collective-permute-done.4
  374.9 4.6 %collective-permute-start.6 = (f32[1]{0:T(128)}, f32[1]{0:T(128)}, u32[]{:S(2)}, u32[]{:S(2)}) collective-permute-start(f32[1]{0:T(128)} %collective-permute-done.4), channel_id=1, source_target_pairs={{0,8},{8,16},{16,24},{24,0},{1,9},{9,17},{17,25},{25,1},{2,10},{10... | collective-permute-start | bytes 20 | tf_op jit(solution)/shard_map/ppermute | solution.py:15
  379.6 0.8 collective-permute-done.6
  380.3 10.4 %collective-permute-done.12 = f32[1,64,4096]{2,1,0:T(8,128)S(1)} collective-permute-done((f32[1,64,4096]{2,1,0:T(8,128)S(1)}, f32[1,64,4096]{2,1,0:T(8,128)S(1)}, u32[]{:S(2)}, u32[]{:S(2)}) %collective-permute-start.12) | collective-permute-done | bytes 1048608 | tf_op jit(solution)/shard_map/ppermute | solution.py:15
  390.8 5.7 %subtract_add_fusion = f32[1,64,4096]{2,1,0:T(8,128)} fusion(f32[1,64,4096]{2,1,0:T(8,128)S(1)} %collective-permute-done.12, f32[1,64,4096]{2,1,0:T(8,128)S(1)} %copy-done.4, f32[1,64,4096]{2,1,0:T(8,128)} %collective-permute-done.7, f32[1,64,4096]{2,1,0:T(8,128)S(1)} %copy-done.3, f32[1,64,4096]{2,1,0:T(8,128)} %collective-permute-done.5, ...), kind=kLoop, calls=%fused_computation.49 | loop fusion | flops 3407872 | bytes 10485776 | tf_op jit(solution)/shard_map/add | solution.py:88
  (39 shorter events, 0.2 us)
Async XLA Ops:
  0.0 25.1 %collective-permute-start.1 = (f32[1,64,4096]{2,1,0:T(8,128)}, f32[1,64,4096]{2,1,0:T(8,128)S(1)}, u32[]{:S(2)}, u32[]{:S(2)}) collective-permute-start(f32[1,64,4096]{2,1,0:T(8,128)} %param.2), channel_id=1, source_target_pairs={{0,1},{1,2},{2,3},{3,4},{4,5},{5,6},{6,7},{7,0},{8,9},{9,10},{10,1... | collective-permute-start | bytes 3145736 | tf_op jit(solution)/shard_map/ppermute | solution.py:15
  25.1 24.0 %copy-start.8 = (f32[1,64,4096]{2,1,0:T(8,128)}, f32[1,64,4096]{2,1,0:T(8,128)S(1)}, u32[]{:S(2)}) copy-start(f32[1,64,4096]{2,1,0:T(8,128)S(1)} %collective-permute-done.1) | copy-start | bytes 3145732
  25.1 24.0 %collective-permute-start.3 = (f32[1,64,4096]{2,1,0:T(8,128)S(1)}, f32[1,64,4096]{2,1,0:T(8,128)S(1)}, u32[]{:S(2)}, u32[]{:S(2)}) collective-permute-start(f32[1,64,4096]{2,1,0:T(8,128)S(1)} %collective-permute-done.1), channel_id=1, source_target_pairs={{0,1},{1,2},{2,3},{3,4},{4,5},{5,6},{6,7},{7,0},{8,9},{9,10},{10,1... | collective-permute-start | bytes 3145736 | tf_op jit(solution)/shard_map/ppermute | solution.py:15
  49.1 2.8 copy-start.10
  107.6 11.3 %copy-start = (f32[1,64,4096]{2,1,0:T(8,128)S(1)}, f32[1,64,4096]{2,1,0:T(8,128)}, u32[]{:S(2)}) copy-start(f32[1,64,4096]{2,1,0:T(8,128)} %param.2) | copy-start | bytes 3145732
  118.9 2.5 copy-start.6
  121.3 26.7 %collective-permute-start.5 = (f32[1,64,4096]{2,1,0:T(8,128)}, f32[1,64,4096]{2,1,0:T(8,128)}, u32[]{:S(2)}, u32[]{:S(2)}) collective-permute-start(f32[1,64,4096]{2,1,0:T(8,128)} %copy-done.10), channel_id=1, source_target_pairs={{0,1},{1,2},{2,3},{3,4},{4,5},{5,6},{6,7},{7,0},{8,9},{9,10},{10,1... | collective-permute-start | bytes 3145736 | tf_op jit(solution)/shard_map/ppermute | solution.py:15
  132.5 55.4 %collective-permute-start.8 = (f32[1,64,4096]{2,1,0:T(8,128)}, f32[1,64,4096]{2,1,0:T(8,128)}, u32[]{:S(2)}, u32[]{:S(2)}) collective-permute-start(f32[1,64,4096]{2,1,0:T(8,128)} %multiply_subtract_fusion.3), channel_id=1, source_target_pairs={{0,1},{1,2},{2,3},{3,4},{4,5},{5,6},{6,7},{7,0},{8,9},{9,10},{10,1... | collective-permute-start | bytes 3145736 | tf_op jit(solution)/shard_map/ppermute | solution.py:15
  148.1 39.8 %collective-permute-start.7 = (f32[1,64,4096]{2,1,0:T(8,128)}, f32[1,64,4096]{2,1,0:T(8,128)}, u32[]{:S(2)}, u32[]{:S(2)}) collective-permute-start(f32[1,64,4096]{2,1,0:T(8,128)} %collective-permute-done.5), channel_id=1, source_target_pairs={{0,8},{8,16},{16,24},{24,0},{1,9},{9,17},{17,25},{25,1},{2,10},{10... | collective-permute-start | bytes 3145736 | tf_op jit(solution)/shard_map/ppermute | solution.py:15
  248.5 8.4 %copy-start.7 = (f32[1,64,4096]{1,2,0:T(8,128)S(1)}, f32[1,64,4096]{1,2,0:T(8,128)}, u32[]{:S(2)}) copy-start(f32[1,64,4096]{1,2,0:T(8,128)} %copy.107) | copy-start | bytes 3145732
  256.9 27.8 %collective-permute-start.9 = (f32[1,64,4096]{2,1,0:T(8,128)}, f32[1,64,4096]{2,1,0:T(8,128)}, u32[]{:S(2)}, u32[]{:S(2)}) collective-permute-start(f32[1,64,4096]{2,1,0:T(8,128)} %get-tuple-element.6), channel_id=1, source_target_pairs={{0,1},{1,2},{2,3},{3,4},{4,5},{5,6},{6,7},{7,0},{8,9},{9,10},{10,1... | collective-permute-start | bytes 3145736 | tf_op jit(solution)/shard_map/ppermute | solution.py:15
  277.5 7.2 %copy-start.2 = (f32[1,64,4096]{2,1,0:T(8,128)S(1)}, f32[1,64,4096]{2,1,0:T(8,128)}, u32[]{:S(2)}) copy-start(f32[1,64,4096]{2,1,0:T(8,128)} %reshape.412) | copy-start | bytes 3145732
  287.1 35.4 %collective-permute-start.10 = (f32[1,64,4096]{2,1,0:T(8,128)}, f32[1,64,4096]{2,1,0:T(8,128)}, u32[]{:S(2)}, u32[]{:S(2)}) collective-permute-start(f32[1,64,4096]{2,1,0:T(8,128)} %multiply_subtract_fusion.1), channel_id=1, source_target_pairs={{0,8},{8,16},{16,24},{24,0},{1,9},{9,17},{17,25},{25,1},{2,10},{10... | collective-permute-start | bytes 3145736 | tf_op jit(solution)/shard_map/ppermute | solution.py:15
  319.5 71.3 %copy-start.1 = (f32[1,64,4096]{2,1,0:T(8,128)S(1)}, f32[1,64,4096]{2,1,0:T(8,128)}, u32[]{:S(2)}) copy-start(f32[1,64,4096]{2,1,0:T(8,128)} %reshape.406) | copy-start | bytes 3145732
  319.5 71.3 %copy-start.3 = (f32[1,64,4096]{2,1,0:T(8,128)S(1)}, f32[1,64,4096]{2,1,0:T(8,128)}, u32[]{:S(2)}) copy-start(f32[1,64,4096]{2,1,0:T(8,128)} %reshape.412) | copy-start | bytes 3145732
  322.5 68.2 %copy-start.4 = (f32[1,64,4096]{2,1,0:T(8,128)S(1)}, f32[1,64,4096]{2,1,0:T(8,128)}, u32[]{:S(2)}) copy-start(f32[1,64,4096]{2,1,0:T(8,128)} %reshape.418) | copy-start | bytes 3145732
  322.5 68.2 %copy-start.5 = (f32[1,64,4096]{2,1,0:T(8,128)S(1)}, f32[1,64,4096]{2,1,0:T(8,128)}, u32[]{:S(2)}) copy-start(f32[1,64,4096]{2,1,0:T(8,128)} %reshape.400) | copy-start | bytes 3145732
  322.5 68.2 %copy-start.9 = (f32[1,64,4096]{2,1,0:T(8,128)S(1)}, f32[1,64,4096]{2,1,0:T(8,128)}, u32[]{:S(2)}) copy-start(f32[1,64,4096]{2,1,0:T(8,128)} %copy-done.8) | copy-start | bytes 3145732
  322.5 68.2 %copy-start.11 = (f32[1,64,4096]{2,1,0:T(8,128)S(1)}, f32[1,64,4096]{2,1,0:T(8,128)}, u32[]{:S(2)}) copy-start(f32[1,64,4096]{2,1,0:T(8,128)} %copy-done.10) | copy-start | bytes 3145732
  324.4 14.3 %collective-permute-start.11 = (f32[1,64,4096]{2,1,0:T(8,128)S(1)}, f32[1,64,4096]{2,1,0:T(8,128)S(1)}, u32[]{:S(2)}, u32[]{:S(2)}) collective-permute-start(f32[1,64,4096]{2,1,0:T(8,128)S(1)} %multiply_subtract_fusion), channel_id=1, source_target_pairs={{0,24},{8,0},{16,8},{24,16},{1,25},{9,1},{17,9},{25,17},{2,26},{10... | collective-permute-start | bytes 3145736 | tf_op jit(solution)/shard_map/ppermute | solution.py:15
  338.7 52.1 %collective-permute-start.12 = (f32[1,64,4096]{2,1,0:T(8,128)S(1)}, f32[1,64,4096]{2,1,0:T(8,128)S(1)}, u32[]{:S(2)}, u32[]{:S(2)}) collective-permute-start(f32[1,64,4096]{2,1,0:T(8,128)S(1)} %collective-permute-done.11), channel_id=1, source_target_pairs={{0,5},{1,6},{2,7},{3,0},{4,1},{5,2},{6,3},{7,4},{8,13},{9,14},{10,... | collective-permute-start | bytes 3145736 | tf_op jit(solution)/shard_map/ppermute | solution.py:15
  347.7 20.6 %collective-permute-start = (f32[1]{0:T(128)}, f32[1]{0:T(128)}, u32[]{:S(2)}, u32[]{:S(2)}) collective-permute-start(f32[1]{0:T(128)} %param.3), channel_id=1, source_target_pairs={{0,1},{1,2},{2,3},{3,4},{4,5},{5,6},{6,7},{7,0},{8,9},{9,10},{10,1... | collective-permute-start | bytes 20 | tf_op jit(solution)/shard_map/ppermute | solution.py:15
  368.3 3.3 collective-permute-start.2
  371.6 3.3 collective-permute-start.4
  374.9 5.4 %collective-permute-start.6 = (f32[1]{0:T(128)}, f32[1]{0:T(128)}, u32[]{:S(2)}, u32[]{:S(2)}) collective-permute-start(f32[1]{0:T(128)} %collective-permute-done.4), channel_id=1, source_target_pairs={{0,8},{8,16},{16,24},{24,0},{1,9},{9,17},{17,25},{25,1},{2,10},{10... | collective-permute-start | bytes 20 | tf_op jit(solution)/shard_map/ppermute | solution.py:15
where the time goes:
time: 403 us; the launch traced here: 397 us
  matrix products  182 us (45%)
  waiting for transfers between devices  98 us (24%)
  local copies, waits for them, and re-layouts  72.7 us (18%)
  starting transfers between devices  22.4 us (6%)
  other arithmetic  20.2 us (5%)
    ppermute x13, waiting for transfers between devices, from_behind(): return lax.ppermute(value, axis, pairs)  98 us
    another operation x8, local copies, waits for them, and re-layouts  49 us
    dot_general x8, matrix products, complex_along(): return jnp.einsum('rskb,spabc->rpakc', table, field, precision=HIGH)  47.9 us
    dot_general x4, matrix products, complex_along(): return jnp.einsum('rska,spabc->rpkbc', table, field, precision=HIGH)  47.3 us
    dot_general x4, matrix products, solve_pairs(): final = jnp.einsum('skc,spabc->pabk', inverse[0], field, precision=HIGH)  33.6 us
    dot_general x4, matrix products, complex_along(): return jnp.einsum('rskc,spabc->rpabk', table, field, precision=HIGH)  28.8 us
    dot_general x4, matrix products, solve_pairs(): jnp.einsum('rka,pabc->rpkbc', forward[:, 0], density, precision=HIGH)  24.6 us
    ppermute x13, starting transfers between devices, from_behind(): return lax.ppermute(value, axis, pairs)  22.4 us
  transfers between devices with their start and end apart: 13, of which 8 were waited for; matrix products, arithmetic and copies ran while one was open for 31% of the time, Pallas kernels for 0%

commit v1 on v0

v1 whole, which is shorter than its diff:
```python
import functools

import jax
import jax.numpy as jnp
import numpy as np
from jax import lax
from jax.experimental import pallas as pl
from jax.experimental.pallas import tpu as pltpu
from jax.sharding import PartitionSpec as P


def real_basis(size):
    x = np.arange(size)
    rows, square = [np.full(size, np.sqrt(1.0 / size))], [0]
    for m in range(1, size // 2):
        angle = 2.0 * np.pi * (m * x % size) / size
        rows.append(np.sqrt(2.0 / size) * np.cos(angle))
        rows.append(np.sqrt(2.0 / size) * np.sin(angle))
        square += [m * m, m * m]
    rows.append(np.sqrt(1.0 / size) * np.where(x % 2 == 0, 1.0, -1.0))
    square.append((size // 2) ** 2)
    return np.stack(rows), np.array(square)


def split(x):
    hi = x.astype(jnp.bfloat16)
    return hi, (x - hi.astype(jnp.float32)).astype(jnp.bfloat16)


def left_table(q):
    hi = q.astype(jnp.bfloat16)
    lo = (q - hi.astype(np.float32)).astype(jnp.bfloat16)
    return np.concatenate([hi, hi, lo], axis=1)


def right_table(q):
    hi = q.astype(jnp.bfloat16)
    lo = (q - hi.astype(np.float32)).astype(jnp.bfloat16)
    return np.concatenate([hi, hi, lo], axis=0)


@functools.cache
def make_tables(size):
    half = size // 2
    basis, square = real_basis(size)
    odd = np.sqrt(square).astype(np.int64) % 2 == 1
    even_rows, odd_rows = np.where(~odd)[0], np.where(odd)[0]
    b_even, b_odd = basis[even_rows][:, :half], basis[odd_rows][:, :half]
    lanes = np.kron(np.array([[1.0, 1.0], [1.0, -1.0]]), basis.T)
    f32 = np.float32
    wl = right_table(lanes.astype(f32))
    wli = right_table(lanes.T.astype(f32))
    b_fwd = left_table(np.concatenate([b_even, b_odd], axis=0).astype(f32))
    b_inv = left_table(np.concatenate([b_even.T, b_odd.T], axis=0).astype(f32))
    a_fwd = left_table(basis.astype(f32))
    a_inv = left_table(basis.T.astype(f32))
    step = 2.0 * np.pi / size
    sq_b = np.stack([square[even_rows], square[odd_rows]], axis=1)
    total = (
        square[None, :, None, None] + sq_b[:, None, :, None] + square[None, None, None, :]
    )
    kern = (np.pi / (step * step * total + 0.25)).astype(f32)
    kern = kern.reshape(half, size, 2 * size)
    return wl, wli, b_fwd, b_inv, a_fwd, a_inv, kern


def stack3(x):
    hi, lo = split(x)
    return jnp.concatenate([hi, lo, hi], axis=0)


def dot(a, b):
    return jnp.dot(a, b, preferred_element_type=jnp.float32)


def pair_body(home, visit, acc_in, acc_out, work, tabs):
    wl, wli, b_fwd, b_inv, a_fwd, a_inv, kern = tabs
    size, half, lanes = home.shape
    block = 8

    def lane_product(x, w):
        hi, lo = split(x)
        return dot(jnp.concatenate([hi, lo, hi], axis=1), w)

    low = lax.broadcasted_iota(jnp.int32, (half, 2 * lanes), 1) % lanes < lanes // 2

    def b_product(rows, table):
        out = []
        for k in range(0, block, 2):
            x = jnp.concatenate(
                [rows[k * half:(k + 1) * half], rows[(k + 1) * half:(k + 2) * half]], axis=1
            )
            y = dot(table, stack3(x))
            y = jnp.where(low, y[:half], y[half:])
            out += [y[:, :lanes], y[:, lanes:]]
        return jnp.concatenate(out, axis=0)

    @pl.loop(0, size // block)
    def _(i):
        at = pl.ds(pl.multiple_of(i * block, block), block)
        x = (home[at] * visit[at]).reshape(block * half, lanes)
        x = lane_product(x, wl[...])
        x = b_product(x, b_fwd[...])
        work[pl.ds(pl.multiple_of(i * block * half, block * half), block * half)] = x

    group = 4

    @pl.loop(0, half // group)
    def _(i):
        x = jnp.concatenate(
            [work[pl.ds(i * group + k, size, stride=half)] for k in range(group)], axis=1
        )
        scale = jnp.concatenate([kern[i * group + k] for k in range(group)], axis=1)
        x = dot(a_fwd[...], stack3(x)) * scale
        x = dot(a_inv[...], stack3(x))
        for k in range(group):
            work[pl.ds(i * group + k, size, stride=half)] = x[:, k * lanes:(k + 1) * lanes]

    @pl.loop(0, size // block)
    def _(i):
        at = pl.ds(pl.multiple_of(i * block, block), block)
        x = work[pl.ds(pl.multiple_of(i * block * half, block * half), block * half)]
        x = b_product(x, b_inv[...])
        x = lane_product(x, wli[...]).reshape(block, half, lanes)
        term = visit[at] * x
        if acc_in is None:
            acc_out[at] = -term
        else:
            acc_out[at] = acc_in[at] - term


def pairs_kernel(count, has_acc, *refs):
    home, visits = refs[0], refs[1:1 + count]
    acc_in = refs[1 + count] if has_acc else None
    tabs = refs[1 + count + has_acc:8 + count + has_acc]
    out, work = refs[8 + count + has_acc:]
    for k in range(count):
        pair_body(home, visits[k], out if k else acc_in, out, work, tabs)


def meet(home, visits, acc, tabs):
    size, half, lanes = home.shape
    count, has_acc = len(visits), int(acc is not None)
    args = [home, *visits] + ([acc] if has_acc else []) + list(tabs)
    return pl.pallas_call(
        functools.partial(pairs_kernel, count, has_acc),
        out_shape=jax.ShapeDtypeStruct(home.shape, jnp.float32),
        in_specs=[pl.BlockSpec(memory_space=pltpu.VMEM)] * len(args),
        out_specs=pl.BlockSpec(memory_space=pltpu.VMEM),
        scratch_shapes=[pltpu.VMEM((size * half, lanes), jnp.float32)],
        compiler_params=pltpu.CompilerParams(vmem_limit_bytes=32 * 2**20),
        cost_estimate=pl.CostEstimate(
            flops=count * 3 * 10**9, bytes_accessed=4 * home.size * (2 + count), transcendentals=0
        ),
    )(*args)


def local(groups, blks, orbitals, occupation):
    size = orbitals.shape[1]
    half = size // 2
    tabs = [jnp.asarray(t) for t in make_tables(size)]
    names = ("group", "blk")
    zs = blks // 2

    def holder(g, b):
        return (g // 2 * 2 + b % 2) * blks + b // 2 * 2 + g % 2

    def send(value, target):
        moves = []
        for g in range(groups):
            for z in range(zs):
                for c in range(2):
                    tg, tz, tc = target(g, z, c)
                    moves.append(
                        (holder(g, 2 * z + c), holder(tg % groups, tz % zs * 2 + tc))
                    )
        return lax.ppermute(value, names, moves)

    swap = [(g * blks + b, holder(g, b)) for g in range(groups) for b in range(blks)]
    core = lax.axis_index("group") % 2

    home = orbitals[0].reshape(size, 2, half, size).transpose(0, 2, 1, 3)
    home = home.reshape(size, half, 2 * size)
    weight = jnp.sqrt(occupation[0])
    home = lax.ppermute(home * weight, names, swap)

    up = send(home, lambda g, z, c: (g, z + 1, c))
    down = send(home, lambda g, z, c: (g, z - 1, c))
    side = send(home, lambda g, z, c: (g, z, 1 - c))
    far = send(
        jnp.where(core == 1, up, down),
        lambda g, z, c: (g, z + (1 if c == 1 else -1), 1 - c),
    )
    up_side = send(up, lambda g, z, c: (g, z, 1 - c))
    down_side = send(down, lambda g, z, c: (g, z, 1 - c))
    cross_near = send(
        jnp.where(core == 0, down_side, up_side),
        lambda g, z, c: (g + (1 if c == 1 else -1), z, c),
    )
    cross_far = send(far, lambda g, z, c: (g + (1 if c == 0 else -1), z, c))

    acc = meet(home, [side], None, tabs)
    acc = meet(home, [up, down], acc, tabs)
    acc = meet(home, [up_side, down_side], acc, tabs)
    acc = meet(home, [far, cross_near], acc, tabs)
    acc = meet(home, [cross_far], acc, tabs)
    acc = lax.ppermute(acc, names, [(t, s) for s, t in swap]) / weight
    acc = acc.reshape(size, half, 2, size).transpose(0, 2, 1, 3)
    return acc.reshape(1, size, size * size)


def solution(mesh):
    return jax.shard_map(
        functools.partial(local, mesh.shape["group"], mesh.shape["blk"]),
        mesh=mesh,
        in_specs=(P(("group", "blk"), None, None), P(("group", "blk"))),
        out_specs=P(("group", "blk"), None, None),
        check_vma=False,
    )
```

time: 403 us -> 170 us (0.42); the launches traced: 397 us -> 168 us
  matrix products: 182 us -> 0 us
  Pallas kernels: 0 us -> 79.6 us
  local copies, waits for them, and re-layouts: 72.7 us -> 13.2 us
  waiting for transfers between devices: 98 us -> 61.5 us
  other arithmetic: 20.2 us -> 3.06 us
  starting transfers between devices: 22.4 us -> 9.79 us
    dot_general x24 -> x0, matrix products: 182 us -> none  [the longest x8 47.9 us: complex_along(): return jnp.einsum('rskb,spabc->rpakc', table, field, precision=HIGH)]
    pallas_call x0 -> x5, Pallas kernels: none -> 79.6 us  [meet(): pl.pallas_call(functools.partial(pairs_kernel, count, has_acc), out_shape...]
    another operation x8 -> x0, local copies, waits for them, and re-layouts: 49 us -> none
    ppermute x13 -> x10, waiting for transfers between devices: 98 us -> 61.5 us  [the longest x8 34.5 us: send(): return lax.ppermute(value, names, moves)]
    ppermute x13 -> x10, starting transfers between devices: 22.4 us -> 9.79 us  [the longest x8 4.02 us: send(): return lax.ppermute(value, names, moves)]
    reshape x4 -> x2, local copies, waits for them, and re-layouts: 12 us -> 4.04 us  [the longest x1 2.88 us: local(): return acc.reshape(1, size, size * size)]
    sub x3 -> x0, other arithmetic: 6.7 us -> none  [collect(): visit_acc - jnp.sum(occupation[:, None, None, None] * orbitals[:, None] *...]
    add x2 -> x0, other arithmetic: 5.8 us -> none  [the longest x1 5.73 us: local(): return home_acc + visit_acc]
  transfers between devices with their start and end apart: 13 -> 10, of which waited for: 8 -> 4; matrix products, arithmetic and copies ran while one was open for 31% -> 1% of each run, Pallas kernels for 0% -> 41%
where the time goes in v1:
time: 170 us; the launch traced here: 168 us
  Pallas kernels  79.6 us (47%)
  waiting for transfers between devices  61.5 us (36%)
  local copies, waits for them, and re-layouts  13.2 us (8%)
  starting transfers between devices  9.79 us (6%)
  other arithmetic  3.06 us (2%)
    pallas_call x5, Pallas kernels, meet(): pl.pallas_call(functools.partial(pairs_kernel, count, has_acc), out_shape...  79.6 us
    ppermute x8, waiting for transfers between devices, send(): return lax.ppermute(value, names, moves)  34.5 us
    ppermute x1, waiting for transfers between devices, local(): acc = lax.ppermute(acc, names, [(t, s) for s, t in swap]) / weight  14.2 us
    ppermute x1, waiting for transfers between devices, local(): home = lax.ppermute(home * weight, names, swap)  12.8 us
    mul x3, local copies, waits for them, and re-layouts, local(): home = lax.ppermute(home * weight, names, swap)  6.65 us
    ppermute x8, starting transfers between devices, send(): return lax.ppermute(value, names, moves)  4.02 us
    ppermute x1, starting transfers between devices, local(): home = lax.ppermute(home * weight, names, swap)  3.84 us
  transfers between devices with their start and end apart: 10, of which 4 were waited for; matrix products, arithmetic and copies ran while one was open for 1% of the time, Pallas kernels for 41%

profile of v1, /device:TPU:9, one launch (start us, length us, event | category | flops | bytes accessed | tf_op | source)
XLA Modules:
  0.0 168.0 jit_solution(5834875008400375031)
XLA Ops:
  0.7 1.3 broadcast_multiply_fusion
  2.0 0.8 mul.19
  2.8 3.2 %copy.13 = f32[64,2,32,64]{3,1,2,0:T(2,128)} copy(f32[64,2,32,64]{3,2,1,0:T(8,128)S(1)} %mul.19) | data formatting | bytes 2097152 | tf_op jit(solution)/shard_map/mul | solution.py:185
  6.1 2.6 %mul.21 = f32[64,32,128]{2,1,0:T(8,128)S(1)} reshape(f32[64,32,2,64]{3,2,1,0:T(2,128)} %bitcast.7) | data formatting | bytes 2097152 | tf_op jit(solution)/shard_map/mul | solution.py:185
  8.7 0.0 copy-start.1
  8.7 0.0 copy-start.2
  8.7 0.0 copy-start.3
  8.7 0.0 copy-start.4
  8.7 0.0 copy-start.5
  8.7 0.0 copy-start.6
  8.7 3.8 %collective-permute-start = (f32[64,32,128]{2,1,0:T(8,128)S(1)}, f32[64,32,128]{2,1,0:T(8,128)}, u32[]{:S(2)}, u32[]{:S(2)}) collective-permute-start(f32[64,32,128]{2,1,0:T(8,128)S(1)} %mul.21), channel_id=1, source_target_pairs={{0,0},{1,8},{2,2},{3,10},{4,4},{5,12},{6,6},{7,14},{8,1},{9,9},{10... | collective-permute-start | bytes 3145736 | tf_op jit(solution)/shard_map/ppermute | solution.py:185
  12.6 12.8 %collective-permute-done.refs_0_ = f32[64,32,128]{2,1,0:T(8,128)} collective-permute-done((f32[64,32,128]{2,1,0:T(8,128)S(1)}, f32[64,32,128]{2,1,0:T(8,128)}, u32[]{:S(2)}, u32[]{:S(2)}) %collective-permute-start) | collective-permute-done | bytes 1048608 | tf_op jit(solution)/shard_map/ppermute | solution.py:185
  25.4 0.2 collective-permute-start.2
  25.5 1.3 collective-permute-start.1
  26.8 0.0 collective-permute-start.8
  26.8 22.2 %collective-permute-done.2.refs_2_ = f32[64,32,128]{2,1,0:T(8,128)S(1)} collective-permute-done((f32[64,32,128]{2,1,0:T(8,128)}, f32[64,32,128]{2,1,0:T(8,128)S(1)}, u32[]{:S(2)}, u32[]{:S(2)}) %collective-permute-start.2) | collective-permute-done | bytes 1048608 | tf_op jit(solution)/shard_map/ppermute | solution.py:177
  49.0 0.0 collective-permute-start.5
  49.0 12.3 %collective-permute-done.1.refs_1_ = f32[64,32,128]{2,1,0:T(8,128)S(1)} collective-permute-done((f32[64,32,128]{2,1,0:T(8,128)}, f32[64,32,128]{2,1,0:T(8,128)S(1)}, u32[]{:S(2)}, u32[]{:S(2)}) %collective-permute-start.1) | collective-permute-done | bytes 1048608 | tf_op jit(solution)/shard_map/ppermute | solution.py:177
  61.3 0.0 collective-permute-start.6
  61.3 0.0 copy-start
  61.3 0.2 broadcast_select_fusion.1
  61.5 0.1 collective-permute-start.3
  61.6 0.0 collective-permute-done.8.refs_1_
  61.6 0.0 copy-done.1
  61.6 0.0 copy-done.2
  61.7 0.0 copy-done.3
  61.7 0.0 copy-done.4
  61.7 0.0 copy-done.5
  61.7 0.0 copy-done.6
  61.7 0.9 copy-done
  62.6 10.6 %shard_map.91.refs_3_ = f32[64,32,128]{2,1,0:T(8,128)S(1)} custom-call(f32[64,32,128]{2,1,0:T(8,128)} %collective-permute-done.refs_0_, f32[64,32,128]{2,1,0:T(8,128)} %collective-permute-done.8.refs_1_, bf16[384,128]{1,0:T(8,128)(2,1)S(1)} %copy-done.1, bf16[384,128]{1,0:T(8,128)(2,1)S(1)} %copy-done.2, bf16[64,96]{1,0:T(8,128)(2,1)S(1)} %copy-done.5, ...), custom_call_target="tpu_custom_call" | custom-call | flops 3000000000 | bytes 3145728 | tf_op jit(solution)/shard_map/pallas_call | solution.py:145
  73.2 0.0 collective-permute-done.5.refs_2_
  73.2 0.0 collective-permute-done.6.refs_1_
  73.2 1.4 broadcast_select_fusion
  74.7 0.8 collective-permute-start.7
  75.5 19.4 %shard_map.92.refs_3_ = f32[64,32,128]{2,1,0:T(8,128)S(1)} custom-call(f32[64,32,128]{2,1,0:T(8,128)} %collective-permute-done.refs_0_, f32[64,32,128]{2,1,0:T(8,128)S(1)} %collective-permute-done.1.refs_1_, f32[64,32,128]{2,1,0:T(8,128)S(1)} %collective-permute-done.2.refs_2_, f32[64,32,128]{2,1,0:T(8,128)S(1)} %shard_map.91.refs_3_, ...), custom_call_target="tpu_custom_call" | custom-call | flops 6000000000 | bytes 4194304 | tf_op jit(solution)/shard_map/pallas_call | solution.py:145
  95.0 0.0 collective-permute-done.3.refs_1_
  95.0 1.6 collective-permute-start.4
  96.6 19.7 %shard_map.93.refs_3_ = f32[64,32,128]{2,1,0:T(8,128)S(1)} custom-call(f32[64,32,128]{2,1,0:T(8,128)} %collective-permute-done.refs_0_, f32[64,32,128]{2,1,0:T(8,128)} %collective-permute-done.6.refs_1_, f32[64,32,128]{2,1,0:T(8,128)S(1)} %collective-permute-done.5.refs_2_, f32[64,32,128]{2,1,0:T(8,128)S(1)} %shard_map.92.refs_3_, ...), custom_call_target="tpu_custom_call" | custom-call | flops 6000000000 | bytes 4194304 | tf_op jit(solution)/shard_map/pallas_call | solution.py:145
  116.3 0.0 collective-permute-done.7.refs_2_
  116.4 19.4 %shard_map.94.refs_2_ = f32[64,32,128]{2,1,0:T(8,128)S(1)} custom-call(f32[64,32,128]{2,1,0:T(8,128)} %collective-permute-done.refs_0_, f32[64,32,128]{2,1,0:T(8,128)S(1)} %collective-permute-done.3.refs_1_, f32[64,32,128]{2,1,0:T(8,128)S(1)} %collective-permute-done.7.refs_2_, f32[64,32,128]{2,1,0:T(8,128)S(1)} %shard_map.93.refs_3_, ...), custom_call_target="tpu_custom_call" | custom-call | flops 6000000000 | bytes 4194304 | tf_op jit(solution)/shard_map/pallas_call | solution.py:145
  135.8 0.0 collective-permute-done.4.refs_1_
  135.8 10.3 %shard_map.95 = f32[64,32,128]{2,1,0:T(8,128)S(1)} custom-call(f32[64,32,128]{2,1,0:T(8,128)} %collective-permute-done.refs_0_, f32[64,32,128]{2,1,0:T(8,128)S(1)} %collective-permute-done.4.refs_1_, f32[64,32,128]{2,1,0:T(8,128)S(1)} %shard_map.94.refs_2_, bf16[384,128]{1,0:T(8,128)(2,1)S(1)} %copy-done.1, bf16[384,128]{1,0:T(8,128)(2,1)S(1)} %copy-done.2, ...), custom_call_target="tpu_custom_call" | custom-call | flops 3000000000 | bytes 3145728 | tf_op jit(solution)/shard_map/pallas_call | solution.py:145
  146.1 1.9 %collective-permute-start.9 = (f32[64,32,128]{2,1,0:T(8,128)S(1)}, f32[64,32,128]{2,1,0:T(8,128)S(1)}, u32[]{:S(2)}, u32[]{:S(2)}) collective-permute-start(f32[64,32,128]{2,1,0:T(8,128)S(1)} %shard_map.95), channel_id=1, source_target_pairs={{0,0},{8,1},{2,2},{10,3},{4,4},{12,5},{6,6},{14,7},{1,8},{9,9},{3,... | collective-permute-start | bytes 3145736 | tf_op jit(solution)/shard_map/ppermute | solution.py:207
  148.1 14.2 %collective-permute-done.9 = f32[64,32,128]{2,1,0:T(8,128)S(1)} collective-permute-done((f32[64,32,128]{2,1,0:T(8,128)S(1)}, f32[64,32,128]{2,1,0:T(8,128)S(1)}, u32[]{:S(2)}, u32[]{:S(2)}) %collective-permute-start.9) | collective-permute-done | bytes 1048608 | tf_op jit(solution)/shard_map/ppermute | solution.py:207
  162.3 0.1 broadcast_divide_fusion
  162.4 1.2 reshape.12
  163.5 1.6 copy.11
  165.1 2.9 %reshape.13 = f32[1,64,4096]{2,1,0:T(8,128)} reshape(f32[64,2,32,64]{3,2,1,0:T(8,128)} %copy.11) | data formatting | bytes 2097152 | tf_op jit(solution)/shard_map/reshape | solution.py:209
Async XLA Ops:
  8.7 53.0 %copy-start.1 = (bf16[384,128]{1,0:T(8,128)(2,1)S(1)}, bf16[384,128]{1,0:T(8,128)(2,1)}, u32[]{:S(2)}) copy-start(bf16[384,128]{1,0:T(8,128)(2,1)} %constant.34.clone.refs_2_.refs_4_.refs_3_) | copy-start | bytes 294916
  8.7 53.0 %copy-start.2 = (bf16[384,128]{1,0:T(8,128)(2,1)S(1)}, bf16[384,128]{1,0:T(8,128)(2,1)}, u32[]{:S(2)}) copy-start(bf16[384,128]{1,0:T(8,128)(2,1)} %constant.35.clone.refs_3_.refs_5_.refs_4_) | copy-start | bytes 294916
  8.7 53.0 %copy-start.3 = (bf16[64,192]{1,0:T(8,128)(2,1)S(1)}, bf16[64,192]{1,0:T(8,128)(2,1)}, u32[]{:S(2)}) copy-start(bf16[64,192]{1,0:T(8,128)(2,1)} %constant.38.clone.refs_6_.refs_8_.refs_7_) | copy-start | bytes 73732
  8.7 53.0 %copy-start.4 = (bf16[64,192]{1,0:T(8,128)(2,1)S(1)}, bf16[64,192]{1,0:T(8,128)(2,1)}, u32[]{:S(2)}) copy-start(bf16[64,192]{1,0:T(8,128)(2,1)} %constant.39.clone.refs_7_.refs_9_.refs_8_) | copy-start | bytes 73732
  8.7 53.0 %copy-start.5 = (bf16[64,96]{1,0:T(8,128)(2,1)S(1)}, bf16[64,96]{1,0:T(8,128)(2,1)}, u32[]{:S(2)}) copy-start(bf16[64,96]{1,0:T(8,128)(2,1)} %constant.36.clone.refs_4_.refs_6_.refs_5_) | copy-start | bytes 36868
  8.7 53.0 %copy-start.6 = (bf16[64,96]{1,0:T(8,128)(2,1)S(1)}, bf16[64,96]{1,0:T(8,128)(2,1)}, u32[]{:S(2)}) copy-start(bf16[64,96]{1,0:T(8,128)(2,1)} %constant.37.clone.refs_5_.refs_7_.refs_6_) | copy-start | bytes 36868
  8.7 16.6 %collective-permute-start = (f32[64,32,128]{2,1,0:T(8,128)S(1)}, f32[64,32,128]{2,1,0:T(8,128)}, u32[]{:S(2)}, u32[]{:S(2)}) collective-permute-start(f32[64,32,128]{2,1,0:T(8,128)S(1)} %mul.21), channel_id=1, source_target_pairs={{0,0},{1,8},{2,2},{3,10},{4,4},{5,12},{6,6},{7,14},{8,1},{9,9},{10... | collective-permute-start | bytes 3145736 | tf_op jit(solution)/shard_map/ppermute | solution.py:185
  25.4 23.6 %collective-permute-start.2 = (f32[64,32,128]{2,1,0:T(8,128)}, f32[64,32,128]{2,1,0:T(8,128)S(1)}, u32[]{:S(2)}, u32[]{:S(2)}) collective-permute-start(f32[64,32,128]{2,1,0:T(8,128)} %collective-permute-done.refs_0_), channel_id=1, source_target_pairs={{0,6},{8,14},{2,0},{10,8},{4,2},{12,10},{6,4},{14,12},{1,7},{9,15}... | collective-permute-start | bytes 3145736 | tf_op jit(solution)/shard_map/ppermute | solution.py:177
  25.5 35.8 %collective-permute-start.1 = (f32[64,32,128]{2,1,0:T(8,128)}, f32[64,32,128]{2,1,0:T(8,128)S(1)}, u32[]{:S(2)}, u32[]{:S(2)}) collective-permute-start(f32[64,32,128]{2,1,0:T(8,128)} %collective-permute-done.refs_0_), channel_id=1, source_target_pairs={{0,2},{8,10},{2,4},{10,12},{4,6},{12,14},{6,0},{14,8},{1,3},{9,11}... | collective-permute-start | bytes 3145736 | tf_op jit(solution)/shard_map/ppermute | solution.py:177
  26.8 34.8 %collective-permute-start.8 = (f32[64,32,128]{2,1,0:T(8,128)}, f32[64,32,128]{2,1,0:T(8,128)}, u32[]{:S(2)}, u32[]{:S(2)}) collective-permute-start(f32[64,32,128]{2,1,0:T(8,128)} %collective-permute-done.refs_0_), channel_id=1, source_target_pairs={{0,8},{8,0},{2,10},{10,2},{4,12},{12,4},{6,14},{14,6},{1,9},{9,1},... | collective-permute-start | bytes 3145736 | tf_op jit(solution)/shard_map/ppermute | solution.py:177
  49.0 24.2 %collective-permute-start.5 = (f32[64,32,128]{2,1,0:T(8,128)S(1)}, f32[64,32,128]{2,1,0:T(8,128)S(1)}, u32[]{:S(2)}, u32[]{:S(2)}) collective-permute-start(f32[64,32,128]{2,1,0:T(8,128)S(1)} %collective-permute-done.2.refs_2_), channel_id=1, source_target_pairs={{0,8},{8,0},{2,10},{10,2},{4,12},{12,4},{6,14},{14,6},{1,9},{9,1},... | collective-permute-start | bytes 3145736 | tf_op jit(solution)/shard_map/ppermute | solution.py:177
  61.3 11.9 %collective-permute-start.6 = (f32[64,32,128]{2,1,0:T(8,128)S(1)}, f32[64,32,128]{2,1,0:T(8,128)}, u32[]{:S(2)}, u32[]{:S(2)}) collective-permute-start(f32[64,32,128]{2,1,0:T(8,128)S(1)} %collective-permute-done.1.refs_1_), channel_id=1, source_target_pairs={{0,8},{8,0},{2,10},{10,2},{4,12},{12,4},{6,14},{14,6},{1,9},{9,1},... | collective-permute-start | bytes 3145736 | tf_op jit(solution)/shard_map/ppermute | solution.py:177
  61.3 1.2 copy-start
  61.5 33.4 %collective-permute-start.3 = (f32[64,32,128]{2,1,0:T(8,128)S(1)}, f32[64,32,128]{2,1,0:T(8,128)S(1)}, u32[]{:S(2)}, u32[]{:S(2)}) collective-permute-start(f32[64,32,128]{2,1,0:T(8,128)S(1)} %broadcast_select_fusion.1), channel_id=1, source_target_pairs={{0,14},{8,2},{2,8},{10,4},{4,10},{12,6},{6,12},{14,0},{1,15},{9,3}... | collective-permute-start | bytes 3145736 | tf_op jit(solution)/shard_map/ppermute | solution.py:177
  74.7 41.7 %collective-permute-start.7 = (f32[64,32,128]{2,1,0:T(8,128)S(1)}, f32[64,32,128]{2,1,0:T(8,128)S(1)}, u32[]{:S(2)}, u32[]{:S(2)}) collective-permute-start(f32[64,32,128]{2,1,0:T(8,128)S(1)} %broadcast_select_fusion), channel_id=1, source_target_pairs={{0,17},{8,9},{2,19},{10,11},{4,21},{12,13},{6,23},{14,15},{1,0},{9... | collective-permute-start | bytes 3145736 | tf_op jit(solution)/shard_map/ppermute | solution.py:177
  95.0 40.8 %collective-permute-start.4 = (f32[64,32,128]{2,1,0:T(8,128)S(1)}, f32[64,32,128]{2,1,0:T(8,128)S(1)}, u32[]{:S(2)}, u32[]{:S(2)}) collective-permute-start(f32[64,32,128]{2,1,0:T(8,128)S(1)} %collective-permute-done.3.refs_1_), channel_id=1, source_target_pairs={{0,1},{8,25},{2,3},{10,27},{4,5},{12,29},{6,7},{14,31},{1,16},{9,8... | collective-permute-start | bytes 3145736 | tf_op jit(solution)/shard_map/ppermute | solution.py:177
  146.1 16.1 %collective-permute-start.9 = (f32[64,32,128]{2,1,0:T(8,128)S(1)}, f32[64,32,128]{2,1,0:T(8,128)S(1)}, u32[]{:S(2)}, u32[]{:S(2)}) collective-permute-start(f32[64,32,128]{2,1,0:T(8,128)S(1)} %shard_map.95), channel_id=1, source_target_pairs={{0,0},{8,1},{2,2},{10,3},{4,4},{12,5},{6,6},{14,7},{1,8},{9,9},{3,... | collective-permute-start | bytes 3145736 | tf_op jit(solution)/shard_map/ppermute | solution.py:207

commit v2 on v1

--- a/solution.py
+++ b/solution.py
@@ -7,6 +7,9 @@
 from jax.experimental import pallas as pl
 from jax.experimental.pallas import tpu as pltpu
 from jax.sharding import PartitionSpec as P
+
+
+BLOCK, GROUP, WIDE = 64, 32, 2
 
 
 def real_basis(size):
@@ -76,23 +79,23 @@
 def pair_body(home, visit, acc_in, acc_out, work, tabs):
     wl, wli, b_fwd, b_inv, a_fwd, a_inv, kern = tabs
     size, half, lanes = home.shape
-    block = 8
+    block = BLOCK
 
     def lane_product(x, w):
         hi, lo = split(x)
         return dot(jnp.concatenate([hi, lo, hi], axis=1), w)
 
-    low = lax.broadcasted_iota(jnp.int32, (half, 2 * lanes), 1) % lanes < lanes // 2
+    low = lax.broadcasted_iota(jnp.int32, (half, WIDE * lanes), 1) % lanes < lanes // 2
 
     def b_product(rows, table):
         out = []
-        for k in range(0, block, 2):
+        for k in range(0, block, WIDE):
             x = jnp.concatenate(
-                [rows[k * half:(k + 1) * half], rows[(k + 1) * half:(k + 2) * half]], axis=1
+                [rows[(k + j) * half:(k + j + 1) * half] for j in range(WIDE)], axis=1
             )
             y = dot(table, stack3(x))
             y = jnp.where(low, y[:half], y[half:])
-            out += [y[:, :lanes], y[:, lanes:]]
+            out += [y[:, j * lanes:(j + 1) * lanes] for j in range(WIDE)]
         return jnp.concatenate(out, axis=0)
 
     @pl.loop(0, size // block)
@@ -103,7 +106,7 @@
         x = b_product(x, b_fwd[...])
         work[pl.ds(pl.multiple_of(i * block * half, block * half), block * half)] = x
 
-    group = 4
+    group = GROUP
 
     @pl.loop(0, half // group)
     def _(i):
@@ -129,30 +132,117 @@
             acc_out[at] = acc_in[at] - term
 
 
-def pairs_kernel(count, has_acc, *refs):
-    home, visits = refs[0], refs[1:1 + count]
-    acc_in = refs[1 + count] if has_acc else None
-    tabs = refs[1 + count + has_acc:8 + count + has_acc]
-    out, work = refs[8 + count + has_acc:]
-    for k in range(count):
-        pair_body(home, visits[k], out if k else acc_in, out, work, tabs)
-
-
-def meet(home, visits, acc, tabs):
+FIRST, SECOND, SIDE, FIRST_SIDE, SECOND_SIDE, FAR, CROSS_NEAR, CROSS_FAR = range(8)
+SLOTS = 8
+
+
+def exchange_kernel(groups, zs, home, *refs):
+    tabs, (out, buf, work, send_sem, recv_sem) = refs[:7], refs[7:]
+    group, blk = lax.axis_index("group"), lax.axis_index("blk")
+    core, z = group % 2, blk // 2
+    g = group // 2 * 2 + blk % 2
+    turn = 2 * core - 1
+
+    def device(tg, tz, tc):
+        tg = (tg + groups) % groups
+        tz = (tz + zs) % zs
+        return (tg // 2 * 2 + tc, tz * 2 + tg % 2)
+
+    goes = {
+        FIRST: device(g, z + turn, core),
+        SECOND: device(g, z - turn, core),
+        SIDE: device(g, z, 1 - core),
+        FIRST_SIDE: device(g, z, 1 - core),
+        SECOND_SIDE: device(g, z, 1 - core),
+        FAR: device(g, z + turn, 1 - core),
+        CROSS_NEAR: device(g + turn, z, core),
+        CROSS_FAR: device(g - turn, z, core),
+    }
+    barrier = pltpu.get_barrier_semaphore()
+    peers = [goes[FIRST], goes[SECOND], goes[SIDE], goes[CROSS_NEAR], goes[CROSS_FAR]]
+    peers += [goes[FAR]]
+    for peer in peers:
+        pl.semaphore_signal(barrier, inc=1, device_id=peer, device_id_type=pl.DeviceIdType.MESH)
+    pl.semaphore_wait(barrier, len(peers))
+
+    def copy(source, slot):
+        return pltpu.make_async_remote_copy(
+            src_ref=source,
+            dst_ref=buf.at[slot],
+            send_sem=send_sem.at[slot],
+            recv_sem=recv_sem.at[slot],
+            device_id=goes[slot],
+            device_id_type=pl.DeviceIdType.MESH,
+        )
+
+    copies = {
+        FIRST: copy(home, FIRST),
+        SECOND: copy(home, SECOND),
+        SIDE: copy(home, SIDE),
+        FIRST_SIDE: copy(buf.at[FIRST], FIRST_SIDE),
+        SECOND_SIDE: copy(buf.at[SECOND], SECOND_SIDE),
+        FAR: copy(buf.at[FIRST], FAR),
+        CROSS_NEAR: copy(buf.at[SECOND_SIDE], CROSS_NEAR),
+        CROSS_FAR: copy(buf.at[FAR], CROSS_FAR),
+    }
+
+    def meet(slot, first=False):
+        pair_body(home, buf.at[slot], None if first else out, out, work, tabs)
+
+    copies[FIRST].start()
+    copies[SIDE].start()
+    copies[SECOND].start()
+    copies[SIDE].wait_recv()
+    meet(SIDE, True)
+    copies[FIRST].wait_recv()
+    copies[FAR].start()
+    copies[FIRST_SIDE].start()
+    meet(FIRST)
+    copies[SECOND].wait_recv()
+    copies[SECOND_SIDE].start()
+    meet(SECOND)
+    copies[SECOND_SIDE].wait_recv()
+    copies[CROSS_NEAR].start()
+    copies[FIRST_SIDE].wait_recv()
+    copies[FAR].wait_recv()
+    copies[CROSS_FAR].start()
+
+    @pl.loop(FIRST_SIDE, CROSS_NEAR)
+    def _(slot):
+        meet(slot)
+
+    copies[CROSS_NEAR].wait_recv()
+    copies[CROSS_FAR].wait_recv()
+
+    @pl.loop(CROSS_NEAR, SLOTS)
+    def _(slot):
+        meet(slot)
+
+    for slot in range(SLOTS):
+        copies[slot].wait_send()
+
+
+def exchange(groups, zs, home, tabs):
     size, half, lanes = home.shape
-    count, has_acc = len(visits), int(acc is not None)
-    args = [home, *visits] + ([acc] if has_acc else []) + list(tabs)
+    vmem = pl.BlockSpec(memory_space=pltpu.VMEM)
     return pl.pallas_call(
-        functools.partial(pairs_kernel, count, has_acc),
+        functools.partial(exchange_kernel, groups, zs),
         out_shape=jax.ShapeDtypeStruct(home.shape, jnp.float32),
-        in_specs=[pl.BlockSpec(memory_space=pltpu.VMEM)] * len(args),
-        out_specs=pl.BlockSpec(memory_space=pltpu.VMEM),
-        scratch_shapes=[pltpu.VMEM((size * half, lanes), jnp.float32)],
-        compiler_params=pltpu.CompilerParams(vmem_limit_bytes=32 * 2**20),
+        in_specs=[vmem] * 8,
+        out_specs=vmem,
+        scratch_shapes=[
+            pltpu.VMEM((SLOTS, size, half, lanes), jnp.float32),
+            pltpu.VMEM((size * half, lanes), jnp.float32),
+            pltpu.SemaphoreType.DMA((SLOTS,)),
+            pltpu.SemaphoreType.DMA((SLOTS,)),
+        ],
+        compiler_params=pltpu.CompilerParams(
+            vmem_limit_bytes=40 * 2**20, collective_id=0, has_side_effects=True
+        ),
         cost_estimate=pl.CostEstimate(
-            flops=count * 3 * 10**9, bytes_accessed=4 * home.size * (2 + count), transcendentals=0
+            flops=24 * 10**9, bytes_accessed=8 * home.size, transcendentals=0
         ),
-    )(*args)
+    )(home, *tabs)
 
 
 def local(groups, blks, orbitals, occupation):
@@ -160,50 +250,16 @@
     half = size // 2
     tabs = [jnp.asarray(t) for t in make_tables(size)]
     names = ("group", "blk")
-    zs = blks // 2
 
     def holder(g, b):
         return (g // 2 * 2 + b % 2) * blks + b // 2 * 2 + g % 2
 
-    def send(value, target):
-        moves = []
-        for g in range(groups):
-            for z in range(zs):
-                for c in range(2):
-                    tg, tz, tc = target(g, z, c)
-                    moves.append(
-                        (holder(g, 2 * z + c), holder(tg % groups, tz % zs * 2 + tc))
-                    )
-        return lax.ppermute(value, names, moves)
-
     swap = [(g * blks + b, holder(g, b)) for g in range(groups) for b in range(blks)]
-    core = lax.axis_index("group") % 2
-
     home = orbitals[0].reshape(size, 2, half, size).transpose(0, 2, 1, 3)
     home = home.reshape(size, half, 2 * size)
     weight = jnp.sqrt(occupation[0])
     home = lax.ppermute(home * weight, names, swap)
-
-    up = send(home, lambda g, z, c: (g, z + 1, c))
-    down = send(home, lambda g, z, c: (g, z - 1, c))
-    side = send(home, lambda g, z, c: (g, z, 1 - c))
-    far = send(
-        jnp.where(core == 1, up, down),
-        lambda g, z, c: (g, z + (1 if c == 1 else -1), 1 - c),
-    )
-    up_side = send(up, lambda g, z, c: (g, z, 1 - c))
-    down_side = send(down, lambda g, z, c: (g, z, 1 - c))
-    cross_near = send(
-        jnp.where(core == 0, down_side, up_side),
-        lambda g, z, c: (g + (1 if c == 1 else -1), z, c),
-    )
-    cross_far = send(far, lambda g, z, c: (g + (1 if c == 0 else -1), z, c))
-
-    acc = meet(home, [side], None, tabs)
-    acc = meet(home, [up, down], acc, tabs)
-    acc = meet(home, [up_side, down_side], acc, tabs)
-    acc = meet(home, [far, cross_near], acc, tabs)
-    acc = meet(home, [cross_far], acc, tabs)
+    acc = exchange(groups, blks // 2, home, tabs)
     acc = lax.ppermute(acc, names, [(t, s) for s, t in swap]) / weight
     acc = acc.reshape(size, half, 2, size).transpose(0, 2, 1, 3)
     return acc.reshape(1, size, size * size)

time: 170 us -> 158 us (0.929)
  waiting for transfers between devices: 61.5 us -> 26.5 us
  Pallas kernels: 79.6 us -> 110 us
  starting transfers between devices: 9.79 us -> 5.81 us
    ppermute x8 -> x0, waiting for transfers between devices: 34.5 us -> none  [send(): return lax.ppermute(value, names, moves)]
    pallas_call x5 -> x1, Pallas kernels: 79.6 us -> 110 us  [exchange(): pl.pallas_call(functools.partial(exchange_kernel, groups, zs), out_shape=...]
    ppermute x8 -> x0, starting transfers between devices: 4.02 us -> none  [send(): return lax.ppermute(value, names, moves)]
  transfers between devices with their start and end apart: 10 -> 2, of which waited for: 4 -> 2; matrix products, arithmetic and copies ran while one was open for 1% -> 0% of each run, Pallas kernels for 41% -> 0%
where the time goes in v2:
time: 158 us; the launch traced here: 157 us
  Pallas kernels  110 us (70%)
  waiting for transfers between devices  26.5 us (17%)
  local copies, waits for them, and re-layouts  12.4 us (8%)
  starting transfers between devices  5.81 us (4%)
    pallas_call x1, Pallas kernels, exchange(): pl.pallas_call(functools.partial(exchange_kernel, groups, zs), out_shape=...  110 us
    ppermute x1, waiting for transfers between devices, local(): acc = lax.ppermute(acc, names, [(t, s) for s, t in swap]) / weight  14.2 us
    ppermute x1, waiting for transfers between devices, local(): home = lax.ppermute(home * weight, names, swap)  12.3 us
    mul x3, local copies, waits for them, and re-layouts, local(): home = lax.ppermute(home * weight, names, swap)  6.76 us
    ppermute x1, starting transfers between devices, local(): home = lax.ppermute(home * weight, names, swap)  3.89 us
  transfers between devices with their start and end apart: 2, of which 2 were waited for; matrix products, arithmetic and copies ran while one was open for 0% of the time, Pallas kernels for 0%

profile of v2, /device:TPU:9, one launch (start us, length us, event | category | flops | bytes accessed | tf_op | source)
XLA Modules:
  0.0 157.2 jit_solution(483095423531199377)
XLA Ops:
  0.7 1.3 broadcast_multiply_fusion
  2.0 0.8 mul.19
  2.8 3.2 %copy.13 = f32[64,2,32,64]{3,1,2,0:T(2,128)} copy(f32[64,2,32,64]{3,2,1,0:T(8,128)S(1)} %mul.19) | data formatting | bytes 2097152 | tf_op jit(solution)/shard_map/mul | solution.py:261
  6.1 0.0 copy-start
  6.1 0.0 copy-start.1
  6.1 0.0 copy-start.2
  6.1 0.0 copy-start.3
  6.1 0.0 copy-start.4
  6.1 0.0 copy-start.5
  6.1 0.0 copy-start.6
  6.1 2.7 %mul.21 = f32[64,32,128]{2,1,0:T(8,128)S(1)} reshape(f32[64,32,2,64]{3,2,1,0:T(2,128)} %bitcast.7) | data formatting | bytes 2097152 | tf_op jit(solution)/shard_map/mul | solution.py:261
  8.8 3.9 %collective-permute-start = (f32[64,32,128]{2,1,0:T(8,128)S(1)}, f32[64,32,128]{2,1,0:T(8,128)S(1)}, u32[]{:S(2)}, u32[]{:S(2)}) collective-permute-start(f32[64,32,128]{2,1,0:T(8,128)S(1)} %mul.21), channel_id=1, source_target_pairs={{0,0},{1,8},{2,2},{3,10},{4,4},{5,12},{6,6},{7,14},{8,1},{9,9},{10... | collective-permute-start | bytes 3145736 | tf_op jit(solution)/shard_map/ppermute | solution.py:261
  12.7 12.3 %collective-permute-done.home = f32[64,32,128]{2,1,0:T(8,128)S(1)} collective-permute-done((f32[64,32,128]{2,1,0:T(8,128)S(1)}, f32[64,32,128]{2,1,0:T(8,128)S(1)}, u32[]{:S(2)}, u32[]{:S(2)}) %collective-permute-start) | collective-permute-done | bytes 1048608 | tf_op jit(solution)/shard_map/ppermute | solution.py:261
  25.0 0.0 copy-done
  25.0 0.0 copy-done.1
  25.0 0.0 copy-done.2
  25.0 0.0 copy-done.3
  25.0 0.0 copy-done.4
  25.0 0.0 copy-done.5
  25.1 0.0 copy-done.6
  25.1 110.2 %shard_map.91 = f32[64,32,128]{2,1,0:T(8,128)S(1)} custom-call(f32[64,32,128]{2,1,0:T(8,128)S(1)} %collective-permute-done.home, bf16[384,128]{1,0:T(8,128)(2,1)S(1)} %copy-done.2, bf16[384,128]{1,0:T(8,128)(2,1)S(1)} %copy-done.1, bf16[64,96]{1,0:T(8,128)(2,1)S(1)} %copy-done.6, bf16[64,96]{1,0:T(8,128)(2,1)S(1)} %copy-done.5, ...), custom_call_target="tpu_custom_call" | custom-call | flops 24000000000 | bytes 2097152 | tf_op jit(solution)/shard_map/pallas_call | solution.py:228
  135.3 1.9 %collective-permute-start.1 = (f32[64,32,128]{2,1,0:T(8,128)S(1)}, f32[64,32,128]{2,1,0:T(8,128)S(1)}, u32[]{:S(2)}, u32[]{:S(2)}) collective-permute-start(f32[64,32,128]{2,1,0:T(8,128)S(1)} %shard_map.91), channel_id=1, source_target_pairs={{0,0},{8,1},{2,2},{10,3},{4,4},{12,5},{6,6},{14,7},{1,8},{9,9},{3,... | collective-permute-start | bytes 3145736 | tf_op jit(solution)/shard_map/ppermute | solution.py:263
  137.2 14.2 %collective-permute-done.1 = f32[64,32,128]{2,1,0:T(8,128)S(1)} collective-permute-done((f32[64,32,128]{2,1,0:T(8,128)S(1)}, f32[64,32,128]{2,1,0:T(8,128)S(1)}, u32[]{:S(2)}, u32[]{:S(2)}) %collective-permute-start.1) | collective-permute-done | bytes 1048608 | tf_op jit(solution)/shard_map/ppermute | solution.py:263
  151.4 0.1 broadcast_divide_fusion
  151.5 1.2 reshape.12
  152.7 1.6 %copy.11 = f32[64,2,32,64]{3,2,1,0:T(8,128)} copy(f32[64,2,32,64]{3,1,2,0:T(2,128)S(1)} %bitcast.8) | data formatting | bytes 2097152 | tf_op jit(solution)/shard_map/transpose | solution.py:264
  154.3 2.9 %reshape.13 = f32[1,64,4096]{2,1,0:T(8,128)} reshape(f32[64,2,32,64]{3,2,1,0:T(8,128)} %copy.11) | data formatting | bytes 2097152 | tf_op jit(solution)/shard_map/reshape | solution.py:265
Async XLA Ops:
  6.1 18.9 %copy-start = (f32[32,64,128]{2,1,0:T(8,128)S(1)}, f32[32,64,128]{2,1,0:T(8,128)}, u32[]{:S(2)}) copy-start(f32[32,64,128]{2,1,0:T(8,128)} %constant.20.clone.refs_6_) | copy-start | bytes 3145732
  6.1 18.9 %copy-start.1 = (bf16[384,128]{1,0:T(8,128)(2,1)S(1)}, bf16[384,128]{1,0:T(8,128)(2,1)}, u32[]{:S(2)}) copy-start(bf16[384,128]{1,0:T(8,128)(2,1)} %constant.15.clone.refs_1_) | copy-start | bytes 294916
  6.1 18.9 %copy-start.2 = (bf16[384,128]{1,0:T(8,128)(2,1)S(1)}, bf16[384,128]{1,0:T(8,128)(2,1)}, u32[]{:S(2)}) copy-start(bf16[384,128]{1,0:T(8,128)(2,1)} %constant.14.clone.refs_0_) | copy-start | bytes 294916
  6.1 18.9 %copy-start.3 = (bf16[64,192]{1,0:T(8,128)(2,1)S(1)}, bf16[64,192]{1,0:T(8,128)(2,1)}, u32[]{:S(2)}) copy-start(bf16[64,192]{1,0:T(8,128)(2,1)} %constant.19.clone.refs_5_) | copy-start | bytes 73732
  6.1 18.9 %copy-start.4 = (bf16[64,192]{1,0:T(8,128)(2,1)S(1)}, bf16[64,192]{1,0:T(8,128)(2,1)}, u32[]{:S(2)}) copy-start(bf16[64,192]{1,0:T(8,128)(2,1)} %constant.18.clone.refs_4_) | copy-start | bytes 73732
  6.1 18.9 %copy-start.5 = (bf16[64,96]{1,0:T(8,128)(2,1)S(1)}, bf16[64,96]{1,0:T(8,128)(2,1)}, u32[]{:S(2)}) copy-start(bf16[64,96]{1,0:T(8,128)(2,1)} %constant.17.clone.refs_3_) | copy-start | bytes 36868
  6.1 18.9 %copy-start.6 = (bf16[64,96]{1,0:T(8,128)(2,1)S(1)}, bf16[64,96]{1,0:T(8,128)(2,1)}, u32[]{:S(2)}) copy-start(bf16[64,96]{1,0:T(8,128)(2,1)} %constant.16.clone.refs_2_) | copy-start | bytes 36868
  8.8 16.2 %collective-permute-start = (f32[64,32,128]{2,1,0:T(8,128)S(1)}, f32[64,32,128]{2,1,0:T(8,128)S(1)}, u32[]{:S(2)}, u32[]{:S(2)}) collective-permute-start(f32[64,32,128]{2,1,0:T(8,128)S(1)} %mul.21), channel_id=1, source_target_pairs={{0,0},{1,8},{2,2},{3,10},{4,4},{5,12},{6,6},{7,14},{8,1},{9,9},{10... | collective-permute-start | bytes 3145736 | tf_op jit(solution)/shard_map/ppermute | solution.py:261
  135.3 16.1 %collective-permute-start.1 = (f32[64,32,128]{2,1,0:T(8,128)S(1)}, f32[64,32,128]{2,1,0:T(8,128)S(1)}, u32[]{:S(2)}, u32[]{:S(2)}) collective-permute-start(f32[64,32,128]{2,1,0:T(8,128)S(1)} %shard_map.91), channel_id=1, source_target_pairs={{0,0},{8,1},{2,2},{10,3},{4,4},{12,5},{6,6},{14,7},{1,8},{9,9},{3,... | collective-permute-start | bytes 3145736 | tf_op jit(solution)/shard_map/ppermute | solution.py:263

commit v3 on v2

--- a/solution.py
+++ b/solution.py
@@ -132,8 +132,9 @@
             acc_out[at] = acc_in[at] - term
 
 
-FIRST, SECOND, SIDE, FIRST_SIDE, SECOND_SIDE, FAR, CROSS_NEAR, CROSS_FAR = range(8)
+SIDE, FIRST, FIRST_SIDE, FAR, SECOND, SECOND_SIDE, CROSS_FAR, CROSS_NEAR = range(8)
 SLOTS = 8
+PARTS = 2
 
 
 def exchange_kernel(groups, zs, home, *refs):
@@ -155,71 +156,90 @@
         FIRST_SIDE: device(g, z, 1 - core),
         SECOND_SIDE: device(g, z, 1 - core),
         FAR: device(g, z + turn, 1 - core),
-        CROSS_NEAR: device(g + turn, z, core),
+        CROSS_NEAR: device(g - turn, z, 1 - core),
         CROSS_FAR: device(g - turn, z, core),
     }
     barrier = pltpu.get_barrier_semaphore()
-    peers = [goes[FIRST], goes[SECOND], goes[SIDE], goes[CROSS_NEAR], goes[CROSS_FAR]]
-    peers += [goes[FAR]]
+    peers = [goes[slot] for slot in (FIRST, SECOND, SIDE, FAR, CROSS_NEAR, CROSS_FAR)]
+    peers.append(device(g + turn, z, core))
     for peer in peers:
         pl.semaphore_signal(barrier, inc=1, device_id=peer, device_id_type=pl.DeviceIdType.MESH)
     pl.semaphore_wait(barrier, len(peers))
 
-    def copy(source, slot):
+    rows = home.shape[0] // PARTS
+
+    def copy(source, slot, part):
+        at = pl.ds(part * rows, rows)
         return pltpu.make_async_remote_copy(
-            src_ref=source,
-            dst_ref=buf.at[slot],
-            send_sem=send_sem.at[slot],
-            recv_sem=recv_sem.at[slot],
+            src_ref=source.at[at],
+            dst_ref=buf.at[slot, at],
+            send_sem=send_sem.at[slot, part],
+            recv_sem=recv_sem.at[slot, part],
             device_id=goes[slot],
             device_id_type=pl.DeviceIdType.MESH,
         )
 
+    sources = {
+        FIRST: home,
+        SECOND: home,
+        SIDE: home,
+        FIRST_SIDE: buf.at[FIRST],
+        SECOND_SIDE: buf.at[SECOND],
+        FAR: buf.at[FIRST],
+        CROSS_NEAR: buf.at[SECOND],
+        CROSS_FAR: buf.at[FAR],
+    }
     copies = {
-        FIRST: copy(home, FIRST),
-        SECOND: copy(home, SECOND),
-        SIDE: copy(home, SIDE),
-        FIRST_SIDE: copy(buf.at[FIRST], FIRST_SIDE),
-        SECOND_SIDE: copy(buf.at[SECOND], SECOND_SIDE),
-        FAR: copy(buf.at[FIRST], FAR),
-        CROSS_NEAR: copy(buf.at[SECOND_SIDE], CROSS_NEAR),
-        CROSS_FAR: copy(buf.at[FAR], CROSS_FAR),
+        slot: [copy(source, slot, part) for part in range(PARTS)]
+        for slot, source in sources.items()
     }
+
+    def start(slot):
+        for part in copies[slot]:
+            part.start()
+
+    def arrive(slot):
+        for part in copies[slot]:
+            part.wait_recv()
+
+    def relay(slot, *onward):
+        for part in range(PARTS):
+            copies[slot][part].wait_recv()
+            for to in onward:
+                copies[to][part].start()
 
     def meet(slot, first=False):
         pair_body(home, buf.at[slot], None if first else out, out, work, tabs)
 
-    copies[FIRST].start()
-    copies[SIDE].start()
-    copies[SECOND].start()
-    copies[SIDE].wait_recv()
+    start(FIRST)
+    start(SIDE)
+    arrive(SIDE)
     meet(SIDE, True)
-    copies[FIRST].wait_recv()
-    copies[FAR].start()
-    copies[FIRST_SIDE].start()
+    relay(FIRST, FAR)
+    start(SECOND)
+    start(FIRST_SIDE)
     meet(FIRST)
-    copies[SECOND].wait_recv()
-    copies[SECOND_SIDE].start()
-    meet(SECOND)
-    copies[SECOND_SIDE].wait_recv()
-    copies[CROSS_NEAR].start()
-    copies[FIRST_SIDE].wait_recv()
-    copies[FAR].wait_recv()
-    copies[CROSS_FAR].start()
-
-    @pl.loop(FIRST_SIDE, CROSS_NEAR)
+    arrive(FIRST_SIDE)
+    meet(FIRST_SIDE)
+    relay(FAR, CROSS_FAR)
+    meet(FAR)
+    relay(SECOND, CROSS_NEAR, SECOND_SIDE)
+    arrive(SECOND_SIDE)
+
+    @pl.loop(SECOND, CROSS_FAR)
     def _(slot):
         meet(slot)
 
-    copies[CROSS_NEAR].wait_recv()
-    copies[CROSS_FAR].wait_recv()
-
-    @pl.loop(CROSS_NEAR, SLOTS)
+    arrive(CROSS_FAR)
+    arrive(CROSS_NEAR)
+
+    @pl.loop(CROSS_FAR, SLOTS)
     def _(slot):
         meet(slot)
 
     for slot in range(SLOTS):
-        copies[slot].wait_send()
+        for part in copies[slot]:
+            part.wait_send()
 
 
 def exchange(groups, zs, home, tabs):
@@ -233,8 +253,8 @@
         scratch_shapes=[
             pltpu.VMEM((SLOTS, size, half, lanes), jnp.float32),
             pltpu.VMEM((size * half, lanes), jnp.float32),
-            pltpu.SemaphoreType.DMA((SLOTS,)),
-            pltpu.SemaphoreType.DMA((SLOTS,)),
+            pltpu.SemaphoreType.DMA((SLOTS, PARTS)),
+            pltpu.SemaphoreType.DMA((SLOTS, PARTS)),
         ],
         compiler_params=pltpu.CompilerParams(
             vmem_limit_bytes=40 * 2**20, collective_id=0, has_side_effects=True

time: 158 us -> 145 us (0.918)
  Pallas kernels: 110 us -> 92.6 us
  starting transfers between devices: 5.81 us -> 13.2 us
  waiting for transfers between devices: 26.5 us -> 24.8 us
    pallas_call x1, Pallas kernels: 110 us -> 92.6 us  [exchange(): pl.pallas_call(functools.partial(exchange_kernel, groups, zs), out_shape=...]
    ppermute x1, starting transfers between devices: 1.92 us -> 9.3 us  [local(): acc = lax.ppermute(acc, names, [(t, s) for s, t in swap]) / weight]
    ppermute x1, waiting for transfers between devices: 14.2 us -> 12.5 us  [local(): acc = lax.ppermute(acc, names, [(t, s) for s, t in swap]) / weight]
where the time goes in v3:
time: 145 us
  Pallas kernels  92.6 us (64%)
  waiting for transfers between devices  24.8 us (17%)
  starting transfers between devices  13.2 us (9%)
  local copies, waits for them, and re-layouts  12.4 us (9%)
    pallas_call x1, Pallas kernels, exchange(): pl.pallas_call(functools.partial(exchange_kernel, groups, zs), out_shape=...  92.6 us
    ppermute x1, waiting for transfers between devices, local(): acc = lax.ppermute(acc, names, [(t, s) for s, t in swap]) / weight  12.5 us
    ppermute x1, waiting for transfers between devices, local(): home = lax.ppermute(home * weight, names, swap)  12.3 us
    ppermute x1, starting transfers between devices, local(): acc = lax.ppermute(acc, names, [(t, s) for s, t in swap]) / weight  9.3 us
    mul x3, local copies, waits for them, and re-layouts, local(): home = lax.ppermute(home * weight, names, swap)  6.76 us
    ppermute x1, starting transfers between devices, local(): home = lax.ppermute(home * weight, names, swap)  3.89 us
  transfers between devices with their start and end apart: 2, of which 2 were waited for; matrix products, arithmetic and copies ran while one was open for 0% of the time, Pallas kernels for 0%

profile of v3, /device:TPU:9, one launch (start us, length us, event | category | flops | bytes accessed | tf_op | source)
XLA Modules:
  0.0 145.2 jit_solution(1904869602033760211)
XLA Ops:
  0.7 1.3 broadcast_multiply_fusion
  2.0 0.8 mul.19
  2.8 3.2 %copy.13 = f32[64,2,32,64]{3,1,2,0:T(2,128)} copy(f32[64,2,32,64]{3,2,1,0:T(8,128)S(1)} %mul.19) | data formatting | bytes 2097152 | tf_op jit(solution)/shard_map/mul | solution.py:281
  6.1 0.0 copy-start
  6.1 0.0 copy-start.1
  6.1 0.0 copy-start.2
  6.1 0.0 copy-start.3
  6.1 0.0 copy-start.4
  6.1 0.0 copy-start.5
  6.1 0.0 copy-start.6
  6.1 2.7 %mul.21 = f32[64,32,128]{2,1,0:T(8,128)S(1)} reshape(f32[64,32,2,64]{3,2,1,0:T(2,128)} %bitcast.7) | data formatting | bytes 2097152 | tf_op jit(solution)/shard_map/mul | solution.py:281
  8.8 3.9 %collective-permute-start = (f32[64,32,128]{2,1,0:T(8,128)S(1)}, f32[64,32,128]{2,1,0:T(8,128)S(1)}, u32[]{:S(2)}, u32[]{:S(2)}) collective-permute-start(f32[64,32,128]{2,1,0:T(8,128)S(1)} %mul.21), channel_id=1, source_target_pairs={{0,0},{1,8},{2,2},{3,10},{4,4},{5,12},{6,6},{7,14},{8,1},{9,9},{10... | collective-permute-start | bytes 3145736 | tf_op jit(solution)/shard_map/ppermute | solution.py:281
  12.7 12.3 %collective-permute-done.home = f32[64,32,128]{2,1,0:T(8,128)S(1)} collective-permute-done((f32[64,32,128]{2,1,0:T(8,128)S(1)}, f32[64,32,128]{2,1,0:T(8,128)S(1)}, u32[]{:S(2)}, u32[]{:S(2)}) %collective-permute-start) | collective-permute-done | bytes 1048608 | tf_op jit(solution)/shard_map/ppermute | solution.py:281
  25.0 0.0 copy-done
  25.0 0.0 copy-done.1
  25.0 0.0 copy-done.2
  25.0 0.0 copy-done.3
  25.0 0.0 copy-done.4
  25.0 0.0 copy-done.5
  25.1 0.0 copy-done.6
  25.1 92.6 %shard_map.91 = f32[64,32,128]{2,1,0:T(8,128)S(1)} custom-call(f32[64,32,128]{2,1,0:T(8,128)S(1)} %collective-permute-done.home, bf16[384,128]{1,0:T(8,128)(2,1)S(1)} %copy-done.2, bf16[384,128]{1,0:T(8,128)(2,1)S(1)} %copy-done.1, bf16[64,96]{1,0:T(8,128)(2,1)S(1)} %copy-done.6, bf16[64,96]{1,0:T(8,128)(2,1)S(1)} %copy-done.5, ...), custom_call_target="tpu_custom_call" | custom-call | flops 24000000000 | bytes 2097152 | tf_op jit(solution)/shard_map/pallas_call | solution.py:248
  117.7 9.3 %collective-permute-start.1 = (f32[64,32,128]{2,1,0:T(8,128)S(1)}, f32[64,32,128]{2,1,0:T(8,128)S(1)}, u32[]{:S(2)}, u32[]{:S(2)}) collective-permute-start(f32[64,32,128]{2,1,0:T(8,128)S(1)} %shard_map.91), channel_id=1, source_target_pairs={{0,0},{8,1},{2,2},{10,3},{4,4},{12,5},{6,6},{14,7},{1,8},{9,9},{3,... | collective-permute-start | bytes 3145736 | tf_op jit(solution)/shard_map/ppermute | solution.py:283
  127.0 12.5 %collective-permute-done.1 = f32[64,32,128]{2,1,0:T(8,128)S(1)} collective-permute-done((f32[64,32,128]{2,1,0:T(8,128)S(1)}, f32[64,32,128]{2,1,0:T(8,128)S(1)}, u32[]{:S(2)}, u32[]{:S(2)}) %collective-permute-start.1) | collective-permute-done | bytes 1048608 | tf_op jit(solution)/shard_map/ppermute | solution.py:283
  139.5 0.1 broadcast_divide_fusion
  139.6 1.2 reshape.12
  140.8 1.6 %copy.11 = f32[64,2,32,64]{3,2,1,0:T(8,128)} copy(f32[64,2,32,64]{3,1,2,0:T(2,128)S(1)} %bitcast.8) | data formatting | bytes 2097152 | tf_op jit(solution)/shard_map/transpose | solution.py:284
  142.4 2.9 %reshape.13 = f32[1,64,4096]{2,1,0:T(8,128)} reshape(f32[64,2,32,64]{3,2,1,0:T(8,128)} %copy.11) | data formatting | bytes 2097152 | tf_op jit(solution)/shard_map/reshape | solution.py:285
Async XLA Ops:
  6.1 18.9 %copy-start = (f32[32,64,128]{2,1,0:T(8,128)S(1)}, f32[32,64,128]{2,1,0:T(8,128)}, u32[]{:S(2)}) copy-start(f32[32,64,128]{2,1,0:T(8,128)} %constant.20.clone.refs_6_) | copy-start | bytes 3145732
  6.1 18.9 %copy-start.1 = (bf16[384,128]{1,0:T(8,128)(2,1)S(1)}, bf16[384,128]{1,0:T(8,128)(2,1)}, u32[]{:S(2)}) copy-start(bf16[384,128]{1,0:T(8,128)(2,1)} %constant.15.clone.refs_1_) | copy-start | bytes 294916
  6.1 18.9 %copy-start.2 = (bf16[384,128]{1,0:T(8,128)(2,1)S(1)}, bf16[384,128]{1,0:T(8,128)(2,1)}, u32[]{:S(2)}) copy-start(bf16[384,128]{1,0:T(8,128)(2,1)} %constant.14.clone.refs_0_) | copy-start | bytes 294916
  6.1 18.9 %copy-start.3 = (bf16[64,192]{1,0:T(8,128)(2,1)S(1)}, bf16[64,192]{1,0:T(8,128)(2,1)}, u32[]{:S(2)}) copy-start(bf16[64,192]{1,0:T(8,128)(2,1)} %constant.19.clone.refs_5_) | copy-start | bytes 73732
  6.1 18.9 %copy-start.4 = (bf16[64,192]{1,0:T(8,128)(2,1)S(1)}, bf16[64,192]{1,0:T(8,128)(2,1)}, u32[]{:S(2)}) copy-start(bf16[64,192]{1,0:T(8,128)(2,1)} %constant.18.clone.refs_4_) | copy-start | bytes 73732
  6.1 18.9 %copy-start.5 = (bf16[64,96]{1,0:T(8,128)(2,1)S(1)}, bf16[64,96]{1,0:T(8,128)(2,1)}, u32[]{:S(2)}) copy-start(bf16[64,96]{1,0:T(8,128)(2,1)} %constant.17.clone.refs_3_) | copy-start | bytes 36868
  6.1 18.9 %copy-start.6 = (bf16[64,96]{1,0:T(8,128)(2,1)S(1)}, bf16[64,96]{1,0:T(8,128)(2,1)}, u32[]{:S(2)}) copy-start(bf16[64,96]{1,0:T(8,128)(2,1)} %constant.16.clone.refs_2_) | copy-start | bytes 36868
  8.8 16.2 %collective-permute-start = (f32[64,32,128]{2,1,0:T(8,128)S(1)}, f32[64,32,128]{2,1,0:T(8,128)S(1)}, u32[]{:S(2)}, u32[]{:S(2)}) collective-permute-start(f32[64,32,128]{2,1,0:T(8,128)S(1)} %mul.21), channel_id=1, source_target_pairs={{0,0},{1,8},{2,2},{3,10},{4,4},{5,12},{6,6},{7,14},{8,1},{9,9},{10... | collective-permute-start | bytes 3145736 | tf_op jit(solution)/shard_map/ppermute | solution.py:281
  117.7 21.8 %collective-permute-start.1 = (f32[64,32,128]{2,1,0:T(8,128)S(1)}, f32[64,32,128]{2,1,0:T(8,128)S(1)}, u32[]{:S(2)}, u32[]{:S(2)}) collective-permute-start(f32[64,32,128]{2,1,0:T(8,128)S(1)} %shard_map.91), channel_id=1, source_target_pairs={{0,0},{8,1},{2,2},{10,3},{4,4},{12,5},{6,6},{14,7},{1,8},{9,9},{3,... | collective-permute-start | bytes 3145736 | tf_op jit(solution)/shard_map/ppermute | solution.py:283
